TPU v7x, 512 devices: a whole 4x4x16 slice. The times are simulated.
512 devices in a mesh: outer: 32 (over x, y, core), inner: 16 (over z).
Axes of the slice: x: 4, y: 4, z: 16, core: 2. Of those that a mesh axis runs over, the one named last changes fastest.
Arguments:
- queries: bfloat16 [65536, 2048], P(('outer', 'inner')), may hold values from -6 to 6
- keys: bfloat16 [65536, 2, 2048], P(('outer', 'inner')), may hold values from -6 to 6
- values: bfloat16 [65536, 2, 2048], P(('outer', 'inner')), may hold values from -6 to 6
- beta_logit: float32 [2, 16, 65536], P(None, None, ('outer', 'inner')), may hold values from -1.5 to 11
- gain: float32 [2048], replicated, may hold values from 0.5 to 1.5
Outputs:
- mixed: bfloat16 [65536, 2048], P(('outer', 'inner'))
All inputs are finite; a program needn't handle non-finite values.
Results may differ from a plain program's by a relative error of at most 0.0045.
Values sent between devices are 32-bit elements; how exact they have to be, the bound alone decides.
No kernel may reach another device: no remote copies, remote signals or barrier semaphores. Data moves between devices by JAX's collectives and lax.ppermute only.
A program may use at most 64 MiB of HBM per device.

v0:
```python
import jax
import jax.numpy as jnp
from jax import lax
from jax.sharding import PartitionSpec as P

HIGH = lax.Precision.HIGHEST


def passed_along(value, axis, by):
    count = lax.axis_size(axis)
    pairs = [(i, i + by) for i in range(count) if 0 <= i + by < count]
    return lax.ppermute(value, axis, pairs)


def unit_rows(field):
    return field / jnp.sqrt(jnp.sum(field * field, axis=-1, keepdims=True) + 1e-06)


def block_terms(queries, keys, values, logits):
    count = queries.shape[0]
    heads = logits.shape[1]
    size = queries.shape[1] // heads
    rows = 2 * count
    qf = unit_rows(queries.astype(jnp.float32).reshape(count, heads, size).transpose(1, 0, 2))
    kf = unit_rows(
        keys.astype(jnp.float32)
        .reshape(count, 2, heads, size)
        .transpose(2, 0, 1, 3)
        .reshape(heads, rows, size)
    )
    vf = (
        values.astype(jnp.float32)
        .reshape(count, 2, heads, size)
        .transpose(2, 0, 1, 3)
        .reshape(heads, rows, size)
    )
    beta = (2.0 * jax.nn.sigmoid(logits)).transpose(1, 2, 0).reshape(heads, rows)
    gram = jnp.einsum("hrd,hsd->hrs", kf, kf, precision=HIGH)
    row_ids = lax.broadcasted_iota(jnp.int32, (rows, rows), 0)
    col_ids = lax.broadcasted_iota(jnp.int32, (rows, rows), 1)
    strict = (row_ids > col_ids)[None]
    eye_rows = jnp.eye(rows, dtype=jnp.float32)[None]
    system = eye_rows + jnp.where(strict, gram * beta[:, None, :], 0.0)
    both = jnp.concatenate([vf, kf], axis=-1)
    solved = lax.linalg.triangular_solve(
        system, both, left_side=True, lower=True, unit_diagonal=True
    )
    fresh = solved[..., :size]
    wmat = solved[..., size:]
    kscaled = kf * beta[:, :, None]
    trans = jnp.eye(size, dtype=jnp.float32)[None] - jnp.einsum(
        "hrd,hre->hde", kscaled, wmat, precision=HIGH
    )
    offset = jnp.einsum("hrd,hre->hde", kscaled, fresh, precision=HIGH)
    scores = jnp.einsum("htd,hsd->hts", qf, kscaled, precision=HIGH)
    tok_ids = lax.broadcasted_iota(jnp.int32, (count, rows), 0)
    virt_ids = lax.broadcasted_iota(jnp.int32, (count, rows), 1)
    scores = jnp.where((virt_ids <= 2 * tok_ids + 1)[None], scores, 0.0)
    local_out = jnp.einsum("hts,hse->hte", scores, fresh, precision=HIGH)
    carried_q = qf - jnp.einsum("hts,hsd->htd", scores, wmat, precision=HIGH)
    return (trans, offset, local_out, carried_q)


def matmul_heads(left, right):
    return jnp.einsum("hde,hef->hdf", left, right, precision=HIGH)


def compose_group(received):
    maps_a = received[0][:, 0]
    maps_b = received[1][:, 0]
    items = maps_a.shape[1]
    size = maps_a.shape[2]
    eye_maps = jnp.broadcast_to(jnp.eye(size, dtype=jnp.float32), (items, size, size))
    zero_maps = jnp.zeros((items, size, size), jnp.float32)

    def step(carry, piece):
        acc_a, acc_b = carry
        piece_a, piece_b = piece
        updated = (matmul_heads(piece_a, acc_a), matmul_heads(piece_a, acc_b) + piece_b)
        return (updated, carry)

    totals, prefixes = lax.scan(step, (eye_maps, zero_maps), (maps_a, maps_b))
    return (prefixes[0], prefixes[1], totals[0][None], totals[1][None])


def local(queries, keys, values, beta_logit, gain):
    trans, offset, local_out, carried_q = block_terms(queries, keys, values, beta_logit)
    heads, size = (trans.shape[0], trans.shape[1])
    n_inner = lax.axis_size("inner")
    owned = heads // n_inner
    trans_split = trans.reshape(1, n_inner, owned, size, size)
    offset_split = offset.reshape(1, n_inner, owned, size, size)
    pre_a, pre_b, tot_a, tot_b = compose_group(
        (
            lax.all_to_all(trans_split, "inner", split_axis=1, concat_axis=0, tiled=True),
            lax.all_to_all(offset_split, "inner", split_axis=1, concat_axis=0, tiled=True),
        )
    )
    tot_a = tot_a[0]
    tot_b = tot_b[0]
    zero_maps = jnp.zeros((owned, size, size), jnp.float32)
    n_outer = lax.axis_size("outer")

    def advance(index, current):
        return passed_along(matmul_heads(tot_a, current) + tot_b, "outer", 1)

    start = lax.fori_loop(0, n_outer - 1, advance, zero_maps)
    entry = jnp.einsum("ihde,hef->ihdf", pre_a, start, precision=HIGH) + pre_b
    entry = lax.all_to_all(entry, "inner", split_axis=0, concat_axis=1, tiled=True)
    state = entry[0]
    outs = local_out + jnp.einsum("htd,hde->hte", carried_q, state, precision=HIGH)
    scale = jnp.sqrt(jnp.mean(outs * outs, axis=-1, keepdims=True) + 1e-06)
    normed = outs / scale * gain.reshape(heads, 1, size)
    count = queries.shape[0]
    return normed.transpose(1, 0, 2).reshape(count, heads * size).astype(jnp.bfloat16)


def solution(mesh):
    return jax.shard_map(
        local,
        mesh=mesh,
        in_specs=(
            P(("outer", "inner"), None),
            P(("outer", "inner"), None, None),
            P(("outer", "inner"), None, None),
            P(None, None, ("outer", "inner")),
            P(),
        ),
        out_specs=P(("outer", "inner"), None),
        check_vma=False,
    )
```

profile of v0, /device:TPU:6, one launch (start us, length us, event | category | flops | bytes accessed | tf_op | source)
XLA Modules:
  0.0 834.4 jit_solution(5811009814303265152)
XLA Ops:
  0.0 3.7 copy_bitcast_fusion.1
  3.7 2.3 fusion.20
  7.0 2.1 broadcast_divide_fusion
  9.1 5.7 select_add_fusion
  14.9 9.4 %while.29 = (s32[]{:T(128)}, f32[16,256,256]{2,1,0:T(8,128)}, s32[2,2]{1,0:T(2,128)S(1)}, f32[2,16,128,128]{3,2,0,1:T(8,128)}, s32[]{:T(128)}) while((s32[]{:T(128)}, f32[16,256,256]{2,1,0:T(8,128)}, s32[2,2]{1,0:T(2,128)S(1)}, f32[2,16,128,128]{3,2,0,1:T(8,128)}, s32[]{:T(128)}) %tuple.53), condition=%wide.while_cond, body=%wide.while_body.sunk | while | flops 2 | bytes 2098785 | solution.py:45
  15.5 4.3 bitcast_dynamic-update-slice_fusion.5
  20.4 3.9 bitcast_dynamic-update-slice_fusion.5
  24.2 315.8 %custom-call.3 = f32[16,2,128,128]{2,3,1,0:T(8,128)} custom-call(f32[16,2,128,128]{3,2,1,0:T(8,128)} %bitcast.171), custom_call_target="InvertDiagBlocksLowerTriangular" | custom-call | tf_op jit(solution)/shard_map/triangular_solve | solution.py:45
  341.7 2.0 fusion.14
  343.7 4.0 fusion.48
  347.6 2.2 fusion.17
  351.2 5.2 fusion.37
  356.4 15.2 %all-to-all-start.1 = ((f32[1,16,1,128,128]{4,3,2,0,1:T(8,128)}), f32[1,16,1,128,128]{4,3,2,0,1:T(8,128)S(1)}, u32[]{:S(2)}, u32[]{:S(2)}) async-start(f32[1,16,1,128,128]{4,3,2,0,1:T(8,128)} %fusion.37), calls=%async_computation.1 | async-start | bytes 2097152 | tf_op jit(solution)/shard_map/all_to_all | solution.py:96
  371.6 6.8 fusion.34
  378.5 43.1 %all-to-all-done.1 = f32[1,16,1,128,128]{4,3,2,0,1:T(8,128)S(1)} async-done(((f32[1,16,1,128,128]{4,3,2,0,1:T(8,128)}), f32[1,16,1,128,128]{4,3,2,0,1:T(8,128)S(1)}, u32[]{:S(2)}, u32[]{:S(2)}) %all-to-all-start.1) | async-done | bytes 1048608 | tf_op jit(solution)/shard_map/all_to_all | solution.py:96
  422.6 7.9 all-to-all-start
  430.5 50.1 %all-to-all-done = f32[1,16,1,128,128]{4,3,2,0,1:T(8,128)S(1)} async-done(((f32[1,16,1,128,128]{4,3,2,0,1:T(8,128)}), f32[1,16,1,128,128]{4,3,2,0,1:T(8,128)S(1)}, u32[]{:S(2)}, u32[]{:S(2)}) %all-to-all-start) | async-done | bytes 1048608 | tf_op jit(solution)/shard_map/all_to_all | solution.py:95
  480.6 42.4 %while.27 = (s32[]{:T(128)}, f32[1,128,128]{2,1,0:T(8,128)S(1)}, f32[1,128,128]{2,1,0:T(8,128)S(1)}, f32[16,1,128,128]{3,2,1,0:T(8,128)}, f32[16,1,128,128]{2,3,...) while((s32[]{:T(128)}, f32[1,128,128]{2,1,0:T(8,128)S(1)}, ...), condition=%wide.region_3.4_spmd, body=%wide.region_2.3_spmd.sunk | while | flops 50348032 | bytes 1116249 | solution.py:82
  523.0 245.1 %while.28 = (s32[]{:T(128)}, f32[1,128,128]{2,1,0:T(8,128)S(1)}, f32[1,128,128]{2,1,0:T(8,128)S(1)}, f32[1,128,128]{2,1,0:T(8,128)S(1)}, s32[]{:T(128)}) while((s32[]{:T(128)}, f32[1,128,128]{2,1,0:T(8,128)S(1)}, f32[1,128,128]{2,1,0:T(8,128)S(1)}, f32[1,128,128]{2,1,0:T(8,128)S(1)}, s32[]{:T(128)}) %tuple.59), condition=%wide.region_5.6_spmd, body=%wide.region_4.5_spmd.sunk | while | flops 25182208 | bytes 524389 | solution.py:107
  525.2 5.8 collective-permute-done
  531.1 1.9 collective-permute-start
  533.1 5.8 collective-permute-done
  539.0 1.9 collective-permute-start
  541.0 5.8 collective-permute-done
  548.9 5.8 collective-permute-done
  556.8 5.8 collective-permute-done
  564.7 5.8 collective-permute-done
  572.6 5.8 collective-permute-done
  580.5 5.8 collective-permute-done
  586.5 1.9 collective-permute-start
  588.4 5.8 collective-permute-done
  596.3 5.8 collective-permute-done
  604.2 5.8 collective-permute-done
  610.2 1.9 collective-permute-start
  612.1 5.8 collective-permute-done
  620.0 5.8 collective-permute-done
  626.0 1.9 collective-permute-start
  627.9 5.8 collective-permute-done
  633.9 1.9 collective-permute-start
  635.8 5.8 collective-permute-done
  643.7 5.8 collective-permute-done
  651.6 5.8 collective-permute-done
  659.5 5.8 collective-permute-done
  667.4 5.8 collective-permute-done
  675.4 5.8 collective-permute-done
  683.3 5.8 collective-permute-done
  691.2 5.8 collective-permute-done
  697.1 1.9 collective-permute-start
  699.1 5.8 collective-permute-done
  707.0 5.8 collective-permute-done
  714.9 5.8 collective-permute-done
  722.8 5.8 collective-permute-done
  730.7 5.8 collective-permute-done
  738.6 5.8 collective-permute-done
  746.5 5.8 collective-permute-done
  754.4 5.8 collective-permute-done
  762.3 5.8 collective-permute-done
  768.1 3.7 fusion.47
  771.8 8.0 all-to-all-start.2
  782.5 3.1 fusion.29
  787.0 3.3 fusion.43
  790.3 33.4 %all-to-all-done.2 = f32[16,1,128,128]{2,3,1,0:T(8,128)} async-done(((f32[16,1,128,128]{2,3,1,0:T(8,128)}), f32[16,1,128,128]{2,3,1,0:T(8,128)}, u32[]{:S(2)}, u32[]{:S(2)}) %all-to-all-start.2) | async-done | bytes 1048608 | tf_op jit(solution)/shard_map/all_to_all | solution.py:109
  823.7 3.8 fusion.52
  827.6 5.4 multiply_reduce_fusion
  (226 shorter events, 105.8 us)
Async XLA Ops:
  0.0 3.7 copy-start.6
  3.7 2.9 copy-start.11
  14.8 325.2 %copy-start.9 = (bf16[128,2,2048]{2,1,0:T(2,128)(2,1)S(1)}, bf16[128,2,2048]{2,1,0:T(2,128)(2,1)}, u32[]{:S(2)}) copy-start(bf16[128,2,2048]{2,1,0:T(2,128)(2,1)} %param.11) | copy-start | bytes 3145732
  340.1 1.6 copy-start.7
  343.7 6.2 copy-start
  349.8 1.3 copy-start.3
  356.4 65.2 %all-to-all-start.1 = ((f32[1,16,1,128,128]{4,3,2,0,1:T(8,128)}), f32[1,16,1,128,128]{4,3,2,0,1:T(8,128)S(1)}, u32[]{:S(2)}, u32[]{:S(2)}) async-start(f32[1,16,1,128,128]{4,3,2,0,1:T(8,128)} %fusion.37), calls=%async_computation.1 | async-start | bytes 2097152 | tf_op jit(solution)/shard_map/all_to_all | solution.py:96
  421.6 1.0 copy-start.8
  422.6 58.0 %all-to-all-start = ((f32[1,16,1,128,128]{4,3,2,0,1:T(8,128)}), f32[1,16,1,128,128]{4,3,2,0,1:T(8,128)S(1)}, u32[]{:S(2)}, u32[]{:S(2)}) async-start(f32[1,16,1,128,128]{4,3,2,0,1:T(8,128)} %fusion.34), calls=%async_computation | async-start | bytes 2097152 | tf_op jit(solution)/shard_map/all_to_all | solution.py:95
  523.2 7.7 collective-permute-start
  531.1 7.7 collective-permute-start
  539.0 7.7 collective-permute-start
  546.9 7.7 collective-permute-start
  554.8 7.7 collective-permute-start
  562.7 7.7 collective-permute-start
  570.7 7.7 collective-permute-start
  578.6 7.7 collective-permute-start
  586.5 7.7 collective-permute-start
  594.4 7.7 collective-permute-start
  602.3 7.7 collective-permute-start
  610.2 7.7 collective-permute-start
  618.1 7.7 collective-permute-start
  626.0 7.7 collective-permute-start
  633.9 7.7 collective-permute-start
  641.8 7.7 collective-permute-start
  649.7 7.7 collective-permute-start
  657.6 7.7 collective-permute-start
  665.5 7.7 collective-permute-start
  673.4 7.7 collective-permute-start
  681.3 7.7 collective-permute-start
  689.2 7.7 collective-permute-start
  697.1 7.7 collective-permute-start
  705.0 7.7 collective-permute-start
  712.9 7.7 collective-permute-start
  720.9 7.7 collective-permute-start
  728.8 7.7 collective-permute-start
  736.7 7.7 collective-permute-start
  744.6 7.7 collective-permute-start
  752.5 7.7 collective-permute-start
  760.4 7.7 collective-permute-start
  768.1 11.7 %copy-start.10 = (bf16[128,2048]{1,0:T(8,128)(2,1)S(1)}, bf16[128,2048]{1,0:T(8,128)(2,1)}, u32[]{:S(2)}) copy-start(bf16[128,2048]{1,0:T(8,128)(2,1)} %param.9) | copy-start | bytes 1572868
  771.8 51.9 %all-to-all-start.2 = ((f32[16,1,128,128]{2,3,1,0:T(8,128)}), f32[16,1,128,128]{2,3,1,0:T(8,128)}, u32[]{:S(2)}, u32[]{:S(2)}) async-start(f32[16,1,128,128]{2,3,1,0:T(8,128)} %fusion.47), calls=%async_computation.2 | async-start | bytes 2097152 | tf_op jit(solution)/shard_map/all_to_all | solution.py:109
  782.5 4.5 copy-start.1
  782.5 4.5 copy-start.4
  785.6 1.3 copy-start.5
  790.3 37.3 %copy-start.2 = (f32[16,128,256]{2,1,0:T(8,128)S(1)}, f32[16,128,256]{2,1,0:T(8,128)}, u32[]{:S(2)}) copy-start(f32[16,128,256]{2,1,0:T(8,128)} %copy-done) | copy-start | bytes 6291460
  827.6 5.5 copy-start.12
where the time goes:
time: 838 us; the launch traced here: 834 us
  other arithmetic  326 us (39%)
  waiting for transfers between devices  305 us (36%)
  starting transfers between devices  90.6 us (11%)
  matrix products  71.6 us (9%)
  local copies, waits for them, and re-layouts  39.5 us (5%)
    another operation x3, other arithmetic, block_terms(): lax.linalg.triangular_solve(system, both, left_side=True, lower=True, uni...  316 us
    ppermute x31, waiting for transfers between devices, passed_along(): return lax.ppermute(value, axis, pairs)  179 us
    ppermute x31, starting transfers between devices, passed_along(): return lax.ppermute(value, axis, pairs)  59.5 us
    all_to_all x1, waiting for transfers between devices, local(): lax.all_to_all(trans_split, 'inner', split_axis=1, concat_axis=0, tiled=T...  50.1 us
    all_to_all x1, waiting for transfers between devices, local(): lax.all_to_all(offset_split, 'inner', split_axis=1, concat_axis=0, tiled=...  43.1 us
    all_to_all x1, waiting for transfers between devices, local(): lax.all_to_all(entry, 'inner', split_axis=0, concat_axis=1, tiled=True)  33.4 us
    dot_general x63, matrix products, matmul_heads(): return jnp.einsum('hde,hef->hdf', left, right, precision=HIGH)  26.3 us
    dynamic_update_slice x48, local copies, waits for them, and re-layouts, compose_group(): totals, prefixes = lax.scan(step, (eye_maps, zero_maps), (maps_a, maps_b))  21.7 us
  transfers between devices with their start and end apart: 34, of which 34 were waited for; matrix products, arithmetic and copies ran while one was open for 2% of the time, Pallas kernels for 0%

commit v1 on v0

v1 whole, which is shorter than its diff:
```python
import jax
import jax.numpy as jnp
from jax import lax
from jax.experimental import pallas as pl
from jax.experimental.pallas import tpu as pltpu
from jax.sharding import Mesh, PartitionSpec as P

F32 = jnp.float32
BF16 = jnp.bfloat16
BASE = 16
GROUP = 128 // BASE
EPS = 1e-06
VMEM = 56 * 1024 * 1024


def parts(x):
    hi = x.astype(BF16)
    lo = (x - hi.astype(F32)).astype(BF16)
    return hi, lo


def dot(a, b):
    return jnp.dot(a, b, preferred_element_type=F32)


def dot_nt(a, b):
    return lax.dot_general(a, b, (((1,), (1,)), ((), ())), preferred_element_type=F32)


def left3(x):
    hi, lo = parts(x)
    return jnp.concatenate([hi, lo], axis=1)


def right3(x):
    hi, lo = parts(x)
    row = jnp.concatenate([hi, lo], axis=1)
    return jnp.concatenate([row, row], axis=0)


def mm3(left, right):
    both = dot(left, right)
    half = both.shape[1] // 2
    return both[:, :half] + both[:, half:]


def iota(shape, dim):
    return lax.broadcasted_iota(jnp.int32, shape, dim)


def reciprocal_root(total):
    y = lax.rsqrt(total)
    return y * (1.5 - 0.5 * total * y * y)


def head_cols(h):
    return slice(h * 128, (h + 1) * 128)


def beta_rows_of(logits):
    heads, count = logits.shape[1], logits.shape[2]
    beta2 = 2.0 / (1.0 + jnp.exp(-logits))
    r_of = iota((count, 2 * count), 1)
    t_of = iota((count, 2 * count), 0)
    beta_rows = jnp.zeros((heads, 2 * count), F32)
    for j in range(2):
        pick = (r_of == 2 * t_of + j).astype(BF16)
        rest = beta2[j]
        for _ in range(3):
            piece = rest.astype(BF16)
            rest = rest - piece.astype(F32)
            beta_rows = beta_rows + dot(piece, pick)
    return beta_rows


def unit_keys(kb):
    kf = kb.astype(F32)
    return kf * reciprocal_root(jnp.sum(kf * kf, axis=1, keepdims=True) + EPS)


def solve_right(rhs, inv, cross):
    z2 = mm3(left3(rhs[:, 128:]), right3(inv[128:]))
    z1 = mm3(left3(rhs[:, :128] - mm3(left3(z2), right3(cross))), right3(inv[:128]))
    return jnp.concatenate([z1, z2], axis=1)


def through_rows(z, kb, vb):
    z_hi, z_lo = parts(z)
    k_hi, k_lo = parts(unit_keys(kb))
    both = jnp.concatenate([k_hi, vb], axis=1)
    prod = dot(z_hi, both) + dot(z_lo, both)
    return prod[:, :128] + dot(z_hi, k_lo), prod[:, 128:]


def maps_kernel(k_ref, v_ref, logit_ref, maps_ref, inv_ref, cross_ref, scale_ref, n_ref, r_ref, c_ref):
    rows = k_ref.shape[0]
    size = 128
    beta_rows = beta_rows_of(logit_ref[...])

    row256 = iota((rows, rows), 0)
    col256 = iota((rows, rows), 1)
    strict = row256 > col256
    diagonal = row256 == col256
    row128 = iota((size, size), 0)
    col128 = iota((size, size), 1)
    eye_b = (row128 == col128).astype(BF16)

    compact = [jnp.zeros((BASE, 128), F32) for _ in range(rows // BASE)]
    lane = iota((BASE, 128), 1)
    for h in range(GROUP):
        kb = k_ref[:, head_cols(h)]
        grams = dot_nt(jnp.concatenate([kb, eye_b], axis=0), kb)
        gram = grams[:rows]
        kf = kb.astype(F32)
        n_col = reciprocal_root(jnp.sum(kf * kf, axis=1, keepdims=True) + EPS)
        n_row = reciprocal_root(jnp.sum(jnp.where(diagonal, gram, 0.0), axis=0, keepdims=True) + EPS)
        scale_row = n_row * beta_rows[h : h + 1, :]
        scale_ref[h : h + 1, :] = scale_row
        system = jnp.where(strict, gram, 0.0) * n_col * scale_row
        n_ref[h] = system
        cross_ref[h] = system[size:, :size]
        r_ref[h] = grams[rows:] * scale_row
        mine = (lane // BASE) == h
        for blk in range(rows // BASE):
            place = blk % GROUP
            tile = blk // GROUP
            slab = system[blk * BASE : (blk + 1) * BASE, tile * 128 : (tile + 1) * 128]
            shift = BASE * ((h - place) % GROUP)
            if shift:
                slab = pltpu.roll(slab, shift, axis=1)
            compact[blk] = jnp.where(mine, slab, compact[blk])

    identity = (iota((BASE, 128), 0) == (lane % BASE)).astype(F32)
    for blk in range(rows // BASE):
        below = compact[blk]
        inv = identity
        for step in range(BASE - 1):
            factor = jnp.take_along_axis(below, (lane // BASE) * BASE + step, axis=1, mode="promise_in_bounds")
            inv = inv - factor * inv[step : step + 1, :]
        c_ref[blk] = inv

    eye = (row128 == col128).astype(F32)
    for h in range(GROUP):
        for tile in range(2):
            pieces = []
            for place in range(GROUP):
                slab = c_ref[tile * GROUP + place]
                shift = BASE * ((place - h) % GROUP)
                if shift:
                    slab = pltpu.roll(slab, shift, axis=1)
                pieces.append(jnp.where((lane // BASE) == place, slab, 0.0))
            inv = jnp.concatenate(pieces, axis=0)
            lower = n_ref[h, tile * 128 : (tile + 1) * 128, tile * 128 : (tile + 1) * 128]
            width = BASE
            while width < size:
                mask = (row128 // (2 * width) == col128 // (2 * width)) & (row128 // width != col128 // width)
                part = jnp.where(mask, lower, 0.0)
                inv_right = right3(inv)
                inv = inv - mm3(left3(inv), right3(mm3(left3(part), inv_right)))
                width *= 2
            inv_ref[h, tile * 128 : (tile + 1) * 128] = inv
        z = solve_right(r_ref[h], inv_ref[h], cross_ref[h])
        through, fresh = through_rows(z, k_ref[:, head_cols(h)], v_ref[:, head_cols(h)])
        maps_ref[h, :, :size] = eye - through
        maps_ref[h, :, size:] = fresh


def block_maps(group, keys, values, logits):
    rows, width = keys.shape
    size = 128
    lanes = GROUP * size
    whole = lambda *shape: pl.BlockSpec(shape, lambda g: (0,) * len(shape))
    return pl.pallas_call(
        maps_kernel,
        grid=(1,),
        in_specs=[
            pl.BlockSpec((rows, lanes), lambda g: (0, group)),
            pl.BlockSpec((rows, lanes), lambda g: (0, group)),
            pl.BlockSpec((2, GROUP, rows // 2), lambda g: (0, group, 0)),
        ],
        out_specs=[
            whole(GROUP, size, 2 * size),
            whole(GROUP, rows, size),
            whole(GROUP, size, size),
            whole(GROUP, rows),
        ],
        out_shape=[
            jax.ShapeDtypeStruct((GROUP, size, 2 * size), F32),
            jax.ShapeDtypeStruct((GROUP, rows, size), F32),
            jax.ShapeDtypeStruct((GROUP, size, size), F32),
            jax.ShapeDtypeStruct((GROUP, rows), F32),
        ],
        scratch_shapes=[
            pltpu.VMEM((GROUP, rows, rows), F32),
            pltpu.VMEM((GROUP, size, rows), F32),
            pltpu.VMEM((rows // BASE, BASE, 128), F32),
        ],
        compiler_params=pltpu.CompilerParams(vmem_limit_bytes=VMEM),
        name="block_maps",
    )(keys, values, logits)


def tokens_kernel(q_ref, k_ref, v_ref, inv_ref, cross_ref, scale_ref, lout_ref, cq_ref):
    count = q_ref.shape[0]
    seen = iota((count, 2 * count), 1) <= 2 * iota((count, 2 * count), 0) + 1
    for h in range(GROUP):
        kb = k_ref[:, head_cols(h)]
        qb = q_ref[:, head_cols(h)]
        scores = jnp.where(seen, dot_nt(qb, kb), 0.0) * scale_ref[h : h + 1, :]
        z = solve_right(scores, inv_ref[h], cross_ref[h])
        through, fresh = through_rows(z, kb, v_ref[:, head_cols(h)])
        qf = qb.astype(F32)
        nq = reciprocal_root(jnp.sum(qf * qf, axis=1, keepdims=True) + EPS)
        cq_ref[h] = nq * (qf - through)
        lout_ref[h] = nq * fresh


def block_tokens(group, queries, keys, values, inv, cross, scale):
    count, width = queries.shape
    rows = 2 * count
    size = 128
    lanes = GROUP * size
    whole = lambda *shape: pl.BlockSpec(shape, lambda g: (0,) * len(shape))
    return pl.pallas_call(
        tokens_kernel,
        grid=(1,),
        in_specs=[
            pl.BlockSpec((count, lanes), lambda g: (0, group)),
            pl.BlockSpec((rows, lanes), lambda g: (0, group)),
            pl.BlockSpec((rows, lanes), lambda g: (0, group)),
            whole(GROUP, rows, size),
            whole(GROUP, size, size),
            whole(GROUP, rows),
        ],
        out_specs=[whole(GROUP, count, size), whole(GROUP, count, size)],
        out_shape=[
            jax.ShapeDtypeStruct((GROUP, count, size), F32),
            jax.ShapeDtypeStruct((GROUP, count, size), F32),
        ],
        compiler_params=pltpu.CompilerParams(vmem_limit_bytes=VMEM),
        name="block_tokens",
    )(queries, keys, values, inv, cross, scale)


def times_map(piece, acc):
    left = left3(piece[:, :128])
    hi, lo = parts(acc)
    return dot(left, jnp.concatenate([hi, hi], axis=0)) + dot(left[:, :128], lo)


def after(piece, acc):
    size = piece.shape[0]
    moved = times_map(piece, acc)
    return jnp.concatenate([moved[:, :size], moved[:, size:] + piece[:, size:]], axis=1)


def advance(piece, state):
    return times_map(piece, state) + piece[:, piece.shape[0] :]


def chain_kernel(maps_ref, total_ref):
    for j in range(maps_ref.shape[1]):
        acc = maps_ref[0, j]
        for i in range(1, maps_ref.shape[0]):
            acc = after(maps_ref[i, j], acc)
        total_ref[j] = acc


def chain(maps, name):
    return pl.pallas_call(
        chain_kernel,
        out_shape=jax.ShapeDtypeStruct(maps.shape[1:], F32),
        compiler_params=pltpu.CompilerParams(vmem_limit_bytes=VMEM),
        name=name,
    )(maps)


def start_kernel(place_ref, by_x_ref, by_y_ref, by_core_ref, quads_ref, entry_ref):
    size = by_x_ref.shape[1]
    state = jnp.zeros((size, size), F32)
    for axis, ref in enumerate((by_x_ref, by_y_ref, by_core_ref)):
        state = lax.fori_loop(0, place_ref[axis], lambda i, s, ref=ref: advance(ref[i], s), state)
    entry_ref[0] = state
    for i in range(quads_ref.shape[0] - 1):
        state = advance(quads_ref[i], state)
        entry_ref[i + 1] = state


def start_states(place, by_x, by_y, by_core, quads):
    count, size, _ = quads.shape
    vmem = pl.BlockSpec(memory_space=pltpu.VMEM)
    return pl.pallas_call(
        start_kernel,
        in_specs=[pl.BlockSpec(memory_space=pltpu.SMEM), vmem, vmem, vmem, vmem],
        out_shape=jax.ShapeDtypeStruct((count, size, size), F32),
        compiler_params=pltpu.CompilerParams(vmem_limit_bytes=VMEM),
        name="start_states",
    )(place, by_x, by_y, by_core, quads)


def spread_kernel(start_ref, first_ref, second_ref, entry_ref):
    members, per = first_ref.shape[0], first_ref.shape[1]
    for j in range(start_ref.shape[0]):
        ref = (first_ref, second_ref)[j // per]
        state = start_ref[j]
        entry_ref[0, j] = state
        for i in range(members - 1):
            state = advance(ref[i, j % per], state)
            entry_ref[i + 1, j] = state


def spread(start, first, second):
    heads, size, _ = start.shape
    return pl.pallas_call(
        spread_kernel,
        out_shape=jax.ShapeDtypeStruct((first.shape[0], heads, size, size), F32),
        compiler_params=pltpu.CompilerParams(vmem_limit_bytes=VMEM),
        name="spread",
    )(start, first, second)


def finish_kernel(lout_ref, cq_ref, state_ref, gain_ref, out_ref):
    for h in range(lout_ref.shape[0]):
        outs = lout_ref[h] + mm3(left3(cq_ref[h]), right3(state_ref[h]))
        total = jnp.mean(outs * outs, axis=1, keepdims=True) + EPS
        normed = outs / jnp.sqrt(total) * gain_ref[:, head_cols(h)]
        out_ref[:, head_cols(h)] = normed.astype(BF16)


def finish(tokens, state, gain):
    (lout0, cq0), (lout1, cq1) = tokens
    count, size = lout0.shape[1], lout0.shape[2]
    members, groups, per = state.shape[0], state.shape[1], state.shape[2]
    heads = members * groups * per

    def kernel(l0, c0, l1, c1, state_ref, gain_ref, out_ref):
        pick = pl.program_id(0) < members

        @pl.when(pick)
        def _():
            finish_kernel(l0, c0, state_ref, gain_ref, out_ref)

        @pl.when(jnp.logical_not(pick))
        def _():
            finish_kernel(l1, c1, state_ref, gain_ref, out_ref)

    low = pl.BlockSpec((per, count, size), lambda g: (jnp.minimum(g, members - 1), 0, 0))
    high = pl.BlockSpec((per, count, size), lambda g: (jnp.maximum(g - members, 0), 0, 0))
    return pl.pallas_call(
        kernel,
        grid=(members * groups,),
        in_specs=[
            low,
            low,
            high,
            high,
            pl.BlockSpec((None, None, per, size, size), lambda g: (g % members, g // members, 0, 0, 0)),
            pl.BlockSpec((1, per * size), lambda g: (0, g)),
        ],
        out_specs=pl.BlockSpec((count, per * size), lambda g: (0, g)),
        out_shape=jax.ShapeDtypeStruct((count, heads * size), BF16),
        compiler_params=pltpu.CompilerParams(vmem_limit_bytes=VMEM),
        name="finish",
    )(lout0, cq0, lout1, cq1, state, gain.reshape(1, heads * size))


def local(queries, keys, values, beta_logit, gain):
    count, width = queries.shape
    keys = keys.reshape(2 * count, width)
    values = values.reshape(2 * count, width)
    quad = lax.axis_size("zi")
    size = 128
    received = []
    saved = []
    for group in range(2):
        maps, inv, cross, scale = block_maps(group, keys, values, beta_logit)
        saved.append((inv, cross, scale))
        got = lax.all_to_all(maps, "zi", split_axis=0, concat_axis=0, tiled=True)
        received.append(got.reshape(quad, GROUP // quad, size, 2 * size))
    tokens = [block_tokens(group, queries, keys, values, *saved[group]) for group in range(2)]
    totals = jnp.concatenate([chain(got, "quad_total") for got in received], axis=0)
    quads = lax.all_to_all(totals, "zq", split_axis=0, concat_axis=0, tiled=True)
    whole = chain(quads[:, None], "group_total")
    by_core = lax.all_gather(whole[0], "core")
    by_y = lax.all_gather(chain(by_core[:, None], "chip_total")[0], "y")
    by_x = lax.all_gather(chain(by_y[:, None], "y_total")[0], "x")
    place = jnp.stack([lax.axis_index("x"), lax.axis_index("y"), lax.axis_index("core")])
    starts = start_states(place, by_x, by_y, by_core, quads)
    mine = lax.all_to_all(starts, "zq", split_axis=0, concat_axis=0, tiled=True)
    entries = spread(mine, received[0], received[1])
    state = lax.all_to_all(entries, "zi", split_axis=0, concat_axis=0, tiled=True)
    state = state.reshape(quad, 2, GROUP // quad, size, size)
    return finish(tokens, state, gain)


def solution(mesh):
    fine = Mesh(mesh.devices.reshape(4, 4, 2, 4, 4), ("x", "y", "core", "zq", "zi"))
    every = ("x", "y", "core", "zq", "zi")
    return jax.shard_map(
        local,
        mesh=fine,
        in_specs=(
            P(every, None),
            P(every, None, None),
            P(every, None, None),
            P(None, None, every),
            P(),
        ),
        out_specs=P(every, None),
        check_vma=False,
    )
```

time: 838 us -> 234 us (0.28)
  other arithmetic: 326 us -> 2.36 us
  waiting for transfers between devices: 305 us -> 61.7 us
  Pallas kernels: 0 us -> 83.3 us
  matrix products: 71.6 us -> 0 us
  starting transfers between devices: 90.6 us -> 25.9 us
  blocking collectives: 0 us -> 52.1 us
  local copies, waits for them, and re-layouts: 39.5 us -> 7.35 us
    another operation x5 -> x1, other arithmetic: 316 us -> 0.58 us  [local(): jnp.stack([lax.axis_index('x'), lax.axis_index('y'), lax.axis_index('core...]
    ppermute x31 -> x0, waiting for transfers between devices: 179 us -> none  [passed_along(): return lax.ppermute(value, axis, pairs)]
    pallas_call x0 -> x12, Pallas kernels: none -> 83.3 us  [the longest x2 42.9 us: block_maps(): pl.pallas_call(maps_kernel, grid=(1,), in_specs=[pl.BlockSpec((rows, lane...]
    all_to_all x3 -> x4, waiting for transfers between devices: 127 us -> 61.7 us  [the longest x1 28.6 us: local(): lax.all_to_all(totals, 'zq', split_axis=0, concat_axis=0, tiled=True)]
    dot_general x71 -> x0, matrix products: 63.4 us -> none  [the longest x63 26.3 us: matmul_heads(): return jnp.einsum('hde,hef->hdf', left, right, precision=HIGH)]
    ppermute x31 -> x0, starting transfers between devices: 59.5 us -> none  [passed_along(): return lax.ppermute(value, axis, pairs)]
    all_gather x0 -> x3, blocking collectives: none -> 33.2 us  [the longest x1 15.4 us: local(): by_y = lax.all_gather(chain(by_core[:, None], 'chip_total')[0], 'y')]
    dynamic_update_slice x48 -> x0, local copies, waits for them, and re-layouts: 21.7 us -> none  [compose_group(): totals, prefixes = lax.scan(step, (eye_maps, zero_maps), (maps_a, maps_b))]
  transfers between devices with their start and end apart: 34 -> 4, of which waited for: 34 -> 4; matrix products, arithmetic and copies ran while one was open for 2% -> 0% of each run, Pallas kernels for 0% -> 17%
where the time goes in v1:
time: 234 us; the launch traced here: 233 us
  Pallas kernels  83.3 us (36%)
  waiting for transfers between devices  61.7 us (26%)
  blocking collectives  52.1 us (22%)
  starting transfers between devices  25.9 us (11%)
  local copies, waits for them, and re-layouts  7.35 us (3%)
  other arithmetic  2.36 us (1%)
    pallas_call x2, Pallas kernels, block_maps(): pl.pallas_call(maps_kernel, grid=(1,), in_specs=[pl.BlockSpec((rows, lane...  42.9 us
    all_to_all x1, waiting for transfers between devices, local(): lax.all_to_all(totals, 'zq', split_axis=0, concat_axis=0, tiled=True)  28.6 us
    all_to_all x2, waiting for transfers between devices, local(): got = lax.all_to_all(maps, 'zi', split_axis=0, concat_axis=0, tiled=True)  26.7 us
    all_to_all x1, blocking collectives, local(): mine = lax.all_to_all(starts, 'zq', split_axis=0, concat_axis=0, tiled=True)  18.9 us
    all_gather x1, blocking collectives, local(): by_y = lax.all_gather(chain(by_core[:, None], 'chip_total')[0], 'y')  15.4 us
    all_gather x1, blocking collectives, local(): by_x = lax.all_gather(chain(by_y[:, None], 'y_total')[0], 'x')  14.4 us
    pallas_call x2, Pallas kernels, block_tokens(): pl.pallas_call(tokens_kernel, grid=(1,), in_specs=[pl.BlockSpec((count, l...  14.4 us
    all_to_all x1, starting transfers between devices, local(): lax.all_to_all(totals, 'zq', split_axis=0, concat_axis=0, tiled=True)  13 us
  transfers between devices with their start and end apart: 4, of which 4 were waited for; matrix products, arithmetic and copies ran while one was open for 0% of the time, Pallas kernels for 17%

profile of v1, /device:TPU:6, one launch (start us, length us, event | category | flops | bytes accessed | tf_op | source)
XLA Modules:
  0.0 232.8 jit_solution(17371016098533157838)
XLA Ops:
  0.0 0.0 copy-start.4
  0.0 2.3 %reshape.18.k_ref = bf16[256,2048]{1,0:T(8,128)(2,1)} reshape(bf16[128,2,2048]{2,1,0:T(2,128)(2,1)} %param.6) | data formatting | bytes 2097152 | tf_op jit(solution)/shard_map/reshape | solution.py:369
  2.3 0.0 copy-done.4
  2.3 1.2 reshape.19.v_ref
  3.6 21.4 %block_maps.3 = (f32[8,128,256]{2,1,0:T(8,128)}, f32[8,256,128]{2,1,0:T(8,128)}, f32[8,128,128]{2,1,0:T(8,128)}, f32[8,256]{1,0:T(8,128)}) custom-call(bf16[256,2048]{1,0:T(8,128)(2,1)} %reshape.18.k_ref, bf16[256,2048]{1,0:T(8,128)(2,1)} %reshape.19.v_ref, f32[2,16,128]{2,1,0:T(8,128)} %logit_ref.3), custom_call_target="tpu_custom_call" | custom-call | tf_op jit(solution)/shard_map/block_maps/pallas_call | solution.py:173
  25.0 5.9 %all-to-all-start.1 = ((f32[8,128,256]{2,1,0:T(8,128)}), f32[8,128,256]{2,1,0:T(8,128)S(1)}, u32[]{:S(2)}, u32[]{:S(2)}) async-start(f32[8,128,256]{2,1,0:T(8,128)} %get-tuple-element.28), calls=%async_computation.1 | async-start | bytes 2097152 | tf_op jit(solution)/shard_map/all_to_all | solution.py:378
  30.9 21.4 %block_maps.2 = (f32[8,128,256]{2,1,0:T(8,128)}, f32[8,256,128]{2,1,0:T(8,128)}, f32[8,128,128]{2,1,0:T(8,128)}, f32[8,256]{1,0:T(8,128)}) custom-call(bf16[256,2048]{1,0:T(8,128)(2,1)} %reshape.18.k_ref, bf16[256,2048]{1,0:T(8,128)(2,1)} %reshape.19.v_ref, f32[2,16,128]{2,1,0:T(8,128)} %logit_ref.3), custom_call_target="tpu_custom_call" | custom-call | tf_op jit(solution)/shard_map/block_maps/pallas_call | solution.py:173
  52.3 4.3 %all-to-all-done.1 = f32[8,128,256]{2,1,0:T(8,128)S(1)} async-done(((f32[8,128,256]{2,1,0:T(8,128)}), f32[8,128,256]{2,1,0:T(8,128)S(1)}, u32[]{:S(2)}, u32[]{:S(2)}) %all-to-all-start.1) | async-done | bytes 1048608 | tf_op jit(solution)/shard_map/all_to_all | solution.py:378
  56.6 0.0 copy-start
  56.6 1.0 copy-done
  57.6 3.5 %all-to-all-start = ((f32[8,128,256]{2,1,0:T(8,128)}), f32[8,128,256]{2,1,0:T(8,128)S(1)}, u32[]{:S(2)}, u32[]{:S(2)}) async-start(f32[8,128,256]{2,1,0:T(8,128)} %get-tuple-element.27), calls=%async_computation | async-start | bytes 2097152 | tf_op jit(solution)/shard_map/all_to_all | solution.py:378
  61.1 2.8 %quad_total.3 = f32[2,128,256]{2,1,0:T(8,128)} custom-call(f32[4,2,128,256]{3,2,1,0:T(8,128)} %bitcast.12), custom_call_target="tpu_custom_call" | custom-call | tf_op jit(solution)/shard_map/quad_total/pallas_call | solution.py:270
  63.9 22.4 %all-to-all-done = f32[8,128,256]{2,1,0:T(8,128)S(1)} async-done(((f32[8,128,256]{2,1,0:T(8,128)}), f32[8,128,256]{2,1,0:T(8,128)S(1)}, u32[]{:S(2)}, u32[]{:S(2)}) %all-to-all-start) | async-done | bytes 1048608 | tf_op jit(solution)/shard_map/all_to_all | solution.py:378
  86.3 0.0 copy-start.1
  86.3 1.0 copy-done.1
  87.3 0.0 copy-start.5
  87.3 2.8 %quad_total.2 = f32[2,128,256]{2,1,0:T(8,128)} custom-call(f32[4,2,128,256]{3,2,1,0:T(8,128)} %bitcast.14), custom_call_target="tpu_custom_call" | custom-call | tf_op jit(solution)/shard_map/quad_total/pallas_call | solution.py:270
  90.2 0.0 copy-done.5
  90.2 1.8 pad_maximum_fusion
  91.9 13.0 %all-to-all-start.2 = ((f32[4,128,256]{2,1,0:T(8,128)}), f32[4,128,256]{2,1,0:T(8,128)S(1)}, u32[]{:S(2)}, u32[]{:S(2)}) async-start(f32[4,128,256]{2,1,0:T(8,128)} %pad_maximum_fusion), calls=%async_computation.2 | async-start | bytes 1048576 | tf_op jit(solution)/shard_map/all_to_all | solution.py:382
  104.9 0.6 pad_add_fusion.place_ref
  105.5 28.6 %all-to-all-done.2.quads_ref = f32[4,128,256]{2,1,0:T(8,128)S(1)} async-done(((f32[4,128,256]{2,1,0:T(8,128)}), f32[4,128,256]{2,1,0:T(8,128)S(1)}, u32[]{:S(2)}, u32[]{:S(2)}) %all-to-all-start.2) | async-done | bytes 524320 | tf_op jit(solution)/shard_map/all_to_all | solution.py:382
  134.1 0.0 copy-start.2
  134.1 0.8 copy-done.2
  134.9 2.3 group_total.1
  137.2 3.5 %all_gather.9.by_core_ref = f32[2,128,256]{2,1,0:T(8,128)} all-gather(f32[1,128,256]{2,1,0:T(8,128)} %group_total.1), channel_id=1, replica_groups=mesh['x'=4,'y'=4,'core'=2,'zq'=4,'zi'=4] {'core'}, dimensions={0}, use_global_device_ids=true | all-gather | bytes 393216 | tf_op jit(solution)/shard_map/all_gather | solution.py:384
  140.7 1.8 chip_total.1
  142.5 15.4 %all_gather.10.by_y_ref = f32[4,128,256]{2,1,0:T(8,128)} all-gather(f32[1,128,256]{2,1,0:T(8,128)} %chip_total.1), channel_id=1, replica_groups=mesh['x'=4,'y'=4,'core'=2,'zq'=4,'zi'=4] {'y'}, dimensions={0}, use_global_device_ids=true | all-gather | bytes 655360 | tf_op jit(solution)/shard_map/all_gather | solution.py:385
  157.8 2.3 y_total.1
  160.1 14.4 %all_gather.11.by_x_ref = f32[4,128,256]{2,1,0:T(8,128)} all-gather(f32[1,128,256]{2,1,0:T(8,128)} %y_total.1), channel_id=1, replica_groups=mesh['x'=4,'y'=4,'core'=2,'zq'=4,'zi'=4] {'x'}, dimensions={0}, use_global_device_ids=true | all-gather | bytes 655360 | tf_op jit(solution)/shard_map/all_gather | solution.py:386
  174.5 3.4 %start_states.1 = f32[4,128,128]{2,1,0:T(8,128)} custom-call(s32[3]{0:T(128)} %pad_add_fusion.place_ref, f32[4,128,256]{2,1,0:T(8,128)} %all_gather.11.by_x_ref, f32[4,128,256]{2,1,0:T(8,128)} %all_gather.10.by_y_ref, f32[2,128,256]{2,1,0:T(8,128)} %all_gather.9.by_core_ref, f32[4,128,256]{2,1,0:T(8,128)} %copy-done.2), custom_call_target="tpu_custom_call" | custom-call | tf_op jit(solution)/shard_map/start_states/pallas_call | solution.py:292
  177.9 18.9 %all_to_all.25.start_ref = f32[4,128,128]{2,1,0:T(8,128)} all-to-all(f32[4,128,128]{2,1,0:T(8,128)} %start_states.1), channel_id=1, replica_groups=mesh['x'=4,'y'=4,'core'=2,'zq'=4,'zi'=4] {'zq'}, dimensions={0} | all-to-all | bytes 524288 | tf_op jit(solution)/shard_map/all_to_all | solution.py:389
  196.8 3.8 %spread.1 = f32[4,4,128,128]{3,2,1,0:T(8,128)} custom-call(f32[4,128,128]{2,1,0:T(8,128)} %all_to_all.25.start_ref, f32[4,2,128,256]{3,2,1,0:T(8,128)} %bitcast.15, f32[4,2,128,256]{3,2,1,0:T(8,128)} %bitcast.13), custom_call_target="tpu_custom_call" | custom-call | tf_op jit(solution)/shard_map/spread/pallas_call | solution.py:314
  200.6 3.5 %all-to-all-start.4 = ((f32[4,4,128,128]{3,2,1,0:T(8,128)}), f32[4,4,128,128]{3,2,1,0:T(8,128)S(1)}, u32[]{:S(2)}, u32[]{:S(2)}) async-start(f32[4,4,128,128]{3,2,1,0:T(8,128)} %spread.1), calls=%async_computation.4 | async-start | bytes 2097152 | tf_op jit(solution)/shard_map/all_to_all | solution.py:391
  204.1 7.2 %block_tokens.2 = (f32[8,128,128]{2,1,0:T(8,128)}, f32[8,128,128]{2,1,0:T(8,128)}) custom-call(bf16[128,2048]{1,0:T(8,128)(2,1)} %q_ref.3, bf16[256,2048]{1,0:T(8,128)(2,1)} %reshape.18.k_ref, bf16[256,2048]{1,0:T(8,128)(2,1)} %reshape.19.v_ref, f32[8,256,128]{2,1,0:T(8,128)} %get-tuple-element.17.inv_ref, f32[8,128,128]{2,1,0:T(8,128)} %get-tuple-element.18.cross_ref, ...), custom_call_target="tpu_custom_call" | custom-call | tf_op jit(solution)/shard_map/block_tokens/pallas_call | solution.py:224
  211.3 7.2 %block_tokens.3 = (f32[8,128,128]{2,1,0:T(8,128)}, f32[8,128,128]{2,1,0:T(8,128)}) custom-call(bf16[128,2048]{1,0:T(8,128)(2,1)} %q_ref.3, bf16[256,2048]{1,0:T(8,128)(2,1)} %reshape.18.k_ref, bf16[256,2048]{1,0:T(8,128)(2,1)} %reshape.19.v_ref, f32[8,256,128]{2,1,0:T(8,128)} %get-tuple-element.22.inv_ref, f32[8,128,128]{2,1,0:T(8,128)} %get-tuple-element.23.cross_ref, ...), custom_call_target="tpu_custom_call" | custom-call | tf_op jit(solution)/shard_map/block_tokens/pallas_call | solution.py:224
  218.5 6.4 %all-to-all-done.4 = f32[4,4,128,128]{3,2,1,0:T(8,128)S(1)} async-done(((f32[4,4,128,128]{3,2,1,0:T(8,128)}), f32[4,4,128,128]{3,2,1,0:T(8,128)S(1)}, u32[]{:S(2)}, u32[]{:S(2)}) %all-to-all-start.4) | async-done | bytes 1048608 | tf_op jit(solution)/shard_map/all_to_all | solution.py:391
  224.9 0.0 copy-start.3
  224.9 1.0 copy-done.3
  225.9 6.9 %finish.1 = bf16[128,2048]{1,0:T(8,128)(2,1)} custom-call(f32[8,128,128]{2,1,0:T(8,128)} %get-tuple-element.20.l0, f32[8,128,128]{2,1,0:T(8,128)} %get-tuple-element.21.c0, f32[8,128,128]{2,1,0:T(8,128)} %get-tuple-element.25.l1, f32[8,128,128]{2,1,0:T(8,128)} %get-tuple-element.26.c1, f32[4,2,2,128,128]{4,3,2,1,0:T(8,128)} %bitcast.18, f32[1,2048]{1,0:T(1,128)} %bitcast.20), custom_call_target="tpu_custom_call" | custom-call | tf_op jit(solution)/shard_map/finish/pallas_call | solution.py:349
Async XLA Ops:
  0.0 2.3 %copy-start.4 = (bf16[128,2,2048]{2,1,0:T(2,128)(2,1)S(1)}, bf16[128,2,2048]{2,1,0:T(2,128)(2,1)}, u32[]{:S(2)}) copy-start(bf16[128,2,2048]{2,1,0:T(2,128)(2,1)} %param.7) | copy-start | bytes 3145732
  25.0 31.6 %all-to-all-start.1 = ((f32[8,128,256]{2,1,0:T(8,128)}), f32[8,128,256]{2,1,0:T(8,128)S(1)}, u32[]{:S(2)}, u32[]{:S(2)}) async-start(f32[8,128,256]{2,1,0:T(8,128)} %get-tuple-element.28), calls=%async_computation.1 | async-start | bytes 2097152 | tf_op jit(solution)/shard_map/all_to_all | solution.py:378
  56.6 1.0 copy-start
  57.6 28.7 %all-to-all-start = ((f32[8,128,256]{2,1,0:T(8,128)}), f32[8,128,256]{2,1,0:T(8,128)S(1)}, u32[]{:S(2)}, u32[]{:S(2)}) async-start(f32[8,128,256]{2,1,0:T(8,128)} %get-tuple-element.27), calls=%async_computation | async-start | bytes 2097152 | tf_op jit(solution)/shard_map/all_to_all | solution.py:378
  86.3 1.0 copy-start.1
  87.3 2.8 %copy-start.5 = (f32[2,128,256]{2,1,0:T(8,128)S(1)}, f32[2,128,256]{2,1,0:T(8,128)}, u32[]{:S(2)}) copy-start(f32[2,128,256]{2,1,0:T(8,128)} %quad_total.3) | copy-start | bytes 786436
  91.9 42.2 %all-to-all-start.2 = ((f32[4,128,256]{2,1,0:T(8,128)}), f32[4,128,256]{2,1,0:T(8,128)S(1)}, u32[]{:S(2)}, u32[]{:S(2)}) async-start(f32[4,128,256]{2,1,0:T(8,128)} %pad_maximum_fusion), calls=%async_computation.2 | async-start | bytes 1048576 | tf_op jit(solution)/shard_map/all_to_all | solution.py:382
  134.1 0.8 copy-start.2
  200.6 24.3 %all-to-all-start.4 = ((f32[4,4,128,128]{3,2,1,0:T(8,128)}), f32[4,4,128,128]{3,2,1,0:T(8,128)S(1)}, u32[]{:S(2)}, u32[]{:S(2)}) async-start(f32[4,4,128,128]{3,2,1,0:T(8,128)} %spread.1), calls=%async_computation.4 | async-start | bytes 2097152 | tf_op jit(solution)/shard_map/all_to_all | solution.py:391
  224.9 1.0 copy-start.3

commit v2 on v1

--- a/solution.py
+++ b/solution.py
@@ -1,3 +1,5 @@
+import functools
+
 import jax
 import jax.numpy as jnp
 from jax import lax
@@ -44,6 +46,9 @@
     return both[:, :half] + both[:, half:]
 
 
+IN_VMEM = pl.BlockSpec(memory_space=pltpu.VMEM)
+
+
 def iota(shape, dim):
     return lax.broadcasted_iota(jnp.int32, shape, dim)
 
@@ -51,6 +56,10 @@
 def reciprocal_root(total):
     y = lax.rsqrt(total)
     return y * (1.5 - 0.5 * total * y * y)
+
+
+def head_rows(ref, h):
+    return ref[:, :, head_cols(h)].reshape(2 * ref.shape[0], 128)
 
 
 def head_cols(h):
@@ -92,8 +101,8 @@
     return prod[:, :128] + dot(z_hi, k_lo), prod[:, 128:]
 
 
-def maps_kernel(k_ref, v_ref, logit_ref, maps_ref, inv_ref, cross_ref, scale_ref, n_ref, r_ref, c_ref):
-    rows = k_ref.shape[0]
+def maps_kernel(k_ref, v_ref, logit_ref, maps_ref, inv_ref, cross_ref, scale_ref, n_ref, r_ref, c_ref, t_ref, z_ref):
+    rows = 2 * k_ref.shape[0]
     size = 128
     beta_rows = beta_rows_of(logit_ref[...])
 
@@ -108,7 +117,7 @@
     compact = [jnp.zeros((BASE, 128), F32) for _ in range(rows // BASE)]
     lane = iota((BASE, 128), 1)
     for h in range(GROUP):
-        kb = k_ref[:, head_cols(h)]
+        kb = head_rows(k_ref, h)
         grams = dot_nt(jnp.concatenate([kb, eye_b], axis=0), kb)
         gram = grams[:rows]
         kf = kb.astype(F32)
@@ -139,34 +148,62 @@
             inv = inv - factor * inv[step : step + 1, :]
         c_ref[blk] = inv
 
-    eye = (row128 == col128).astype(F32)
     for h in range(GROUP):
         for tile in range(2):
-            pieces = []
             for place in range(GROUP):
                 slab = c_ref[tile * GROUP + place]
                 shift = BASE * ((place - h) % GROUP)
                 if shift:
                     slab = pltpu.roll(slab, shift, axis=1)
-                pieces.append(jnp.where((lane // BASE) == place, slab, 0.0))
-            inv = jnp.concatenate(pieces, axis=0)
-            lower = n_ref[h, tile * 128 : (tile + 1) * 128, tile * 128 : (tile + 1) * 128]
-            width = BASE
-            while width < size:
-                mask = (row128 // (2 * width) == col128 // (2 * width)) & (row128 // width != col128 // width)
-                part = jnp.where(mask, lower, 0.0)
-                inv_right = right3(inv)
-                inv = inv - mm3(left3(inv), right3(mm3(left3(part), inv_right)))
-                width *= 2
-            inv_ref[h, tile * 128 : (tile + 1) * 128] = inv
-        z = solve_right(r_ref[h], inv_ref[h], cross_ref[h])
-        through, fresh = through_rows(z, k_ref[:, head_cols(h)], v_ref[:, head_cols(h)])
+                first = tile * 128 + place * BASE
+                inv_ref[h, first : first + BASE] = jnp.where((lane // BASE) == place, slab, 0.0)
+    width = BASE
+    while width < size:
+        odd = range(width, size, 2 * width)
+        mask = col128[:width] // width
+        for h in range(GROUP):
+            for tile in range(2):
+                base = tile * 128
+                inv = inv_ref[h, base : base + 128]
+                part = jnp.concatenate(
+                    [
+                        jnp.where(mask == at // width - 1, n_ref[h, base + at : base + at + width, base : base + 128], 0.0)
+                        for at in odd
+                    ],
+                    axis=0,
+                )
+                t_ref[h, tile] = mm3(left3(part), right3(inv))
+        for h in range(GROUP):
+            for tile in range(2):
+                base = tile * 128
+                own = jnp.concatenate([inv_ref[h, base + at : base + at + width] for at in odd], axis=0)
+                hi, lo = parts(t_ref[h, tile])
+                both = jnp.concatenate([hi, lo], axis=1)
+                none = jnp.zeros((width, 256), BF16)
+                spread = []
+                for i in range(len(odd)):
+                    spread += [none, both[i * width : (i + 1) * width]]
+                spread = jnp.concatenate(spread, axis=0)
+                new = own - mm3(left3(own), jnp.concatenate([spread, spread], axis=0))
+                for i, at in enumerate(odd):
+                    inv_ref[h, base + at : base + at + width] = new[i * width : (i + 1) * width]
+        width *= 2
+
+    eye = (row128 == col128).astype(F32)
+    for h in range(GROUP):
+        z_ref[h, :, size:] = mm3(left3(r_ref[h, :, size:]), right3(inv_ref[h, size:]))
+    for h in range(GROUP):
+        r_ref[h, :, :size] = r_ref[h, :, :size] - mm3(left3(z_ref[h, :, size:]), right3(cross_ref[h]))
+    for h in range(GROUP):
+        z_ref[h, :, :size] = mm3(left3(r_ref[h, :, :size]), right3(inv_ref[h, :size]))
+    for h in range(GROUP):
+        through, fresh = through_rows(z_ref[h], head_rows(k_ref, h), head_rows(v_ref, h))
         maps_ref[h, :, :size] = eye - through
         maps_ref[h, :, size:] = fresh
 
 
 def block_maps(group, keys, values, logits):
-    rows, width = keys.shape
+    rows = 2 * keys.shape[0]
     size = 128
     lanes = GROUP * size
     whole = lambda *shape: pl.BlockSpec(shape, lambda g: (0,) * len(shape))
@@ -174,8 +211,8 @@
         maps_kernel,
         grid=(1,),
         in_specs=[
-            pl.BlockSpec((rows, lanes), lambda g: (0, group)),
-            pl.BlockSpec((rows, lanes), lambda g: (0, group)),
+            pl.BlockSpec((rows // 2, 2, lanes), lambda g: (0, 0, group)),
+            pl.BlockSpec((rows // 2, 2, lanes), lambda g: (0, 0, group)),
             pl.BlockSpec((2, GROUP, rows // 2), lambda g: (0, group, 0)),
         ],
         out_specs=[
@@ -194,6 +231,8 @@
             pltpu.VMEM((GROUP, rows, rows), F32),
             pltpu.VMEM((GROUP, size, rows), F32),
             pltpu.VMEM((rows // BASE, BASE, 128), F32),
+            pltpu.VMEM((GROUP, 2, size // 2, size), F32),
+            pltpu.VMEM((GROUP, size, rows), F32),
         ],
         compiler_params=pltpu.CompilerParams(vmem_limit_bytes=VMEM),
         name="block_maps",
@@ -204,11 +243,11 @@
     count = q_ref.shape[0]
     seen = iota((count, 2 * count), 1) <= 2 * iota((count, 2 * count), 0) + 1
     for h in range(GROUP):
-        kb = k_ref[:, head_cols(h)]
+        kb = head_rows(k_ref, h)
         qb = q_ref[:, head_cols(h)]
         scores = jnp.where(seen, dot_nt(qb, kb), 0.0) * scale_ref[h : h + 1, :]
         z = solve_right(scores, inv_ref[h], cross_ref[h])
-        through, fresh = through_rows(z, kb, v_ref[:, head_cols(h)])
+        through, fresh = through_rows(z, kb, head_rows(v_ref, h))
         qf = qb.astype(F32)
         nq = reciprocal_root(jnp.sum(qf * qf, axis=1, keepdims=True) + EPS)
         cq_ref[h] = nq * (qf - through)
@@ -226,8 +265,8 @@
         grid=(1,),
         in_specs=[
             pl.BlockSpec((count, lanes), lambda g: (0, group)),
-            pl.BlockSpec((rows, lanes), lambda g: (0, group)),
-            pl.BlockSpec((rows, lanes), lambda g: (0, group)),
+            pl.BlockSpec((rows // 2, 2, lanes), lambda g: (0, 0, group)),
+            pl.BlockSpec((rows // 2, 2, lanes), lambda g: (0, 0, group)),
             whole(GROUP, rows, size),
             whole(GROUP, size, size),
             whole(GROUP, rows),
@@ -258,21 +297,30 @@
     return times_map(piece, state) + piece[:, piece.shape[0] :]
 
 
-def chain_kernel(maps_ref, total_ref):
-    for j in range(maps_ref.shape[1]):
-        acc = maps_ref[0, j]
-        for i in range(1, maps_ref.shape[0]):
-            acc = after(maps_ref[i, j], acc)
-        total_ref[j] = acc
-
-
-def chain(maps, name):
-    return pl.pallas_call(
-        chain_kernel,
-        out_shape=jax.ShapeDtypeStruct(maps.shape[1:], F32),
+def chain_kernel(pieces, maps_ref, *refs):
+    total_ref = refs[-1]
+    heads = maps_ref.shape[0] // pieces
+    done = 0
+    for earlier in refs[:-1]:
+        done = earlier.shape[0]
+        total_ref[:done] = earlier[...]
+    accs = [maps_ref[j] for j in range(heads)]
+    for i in range(1, pieces):
+        accs = [after(maps_ref[i * heads + j], acc) for j, acc in enumerate(accs)]
+    for j, acc in enumerate(accs):
+        total_ref[done + j] = acc
+
+
+def chain(name, pieces, maps, *earlier):
+    count = maps.shape[0] // pieces + sum(part.shape[0] for part in earlier)
+    return pl.pallas_call(
+        functools.partial(chain_kernel, pieces),
+        in_specs=[IN_VMEM] * (1 + len(earlier)),
+        out_specs=IN_VMEM,
+        out_shape=jax.ShapeDtypeStruct((count,) + maps.shape[1:], F32),
         compiler_params=pltpu.CompilerParams(vmem_limit_bytes=VMEM),
         name=name,
-    )(maps)
+    )(maps, *earlier)
 
 
 def start_kernel(place_ref, by_x_ref, by_y_ref, by_core_ref, quads_ref, entry_ref):
@@ -288,10 +336,10 @@
 
 def start_states(place, by_x, by_y, by_core, quads):
     count, size, _ = quads.shape
-    vmem = pl.BlockSpec(memory_space=pltpu.VMEM)
     return pl.pallas_call(
         start_kernel,
-        in_specs=[pl.BlockSpec(memory_space=pltpu.SMEM), vmem, vmem, vmem, vmem],
+        in_specs=[pl.BlockSpec(memory_space=pltpu.SMEM)] + [IN_VMEM] * 4,
+        out_specs=IN_VMEM,
         out_shape=jax.ShapeDtypeStruct((count, size, size), F32),
         compiler_params=pltpu.CompilerParams(vmem_limit_bytes=VMEM),
         name="start_states",
@@ -299,65 +347,77 @@
 
 
 def spread_kernel(start_ref, first_ref, second_ref, entry_ref):
-    members, per = first_ref.shape[0], first_ref.shape[1]
-    for j in range(start_ref.shape[0]):
-        ref = (first_ref, second_ref)[j // per]
-        state = start_ref[j]
-        entry_ref[0, j] = state
-        for i in range(members - 1):
-            state = advance(ref[i, j % per], state)
-            entry_ref[i + 1, j] = state
+    heads = start_ref.shape[0]
+    per = heads // 2
+    members = first_ref.shape[0] // per
+    states = [start_ref[j] for j in range(heads)]
+    for i in range(members):
+        for j in range(heads):
+            entry_ref[i * heads + j] = states[j]
+        if i < members - 1:
+            states = [advance((first_ref, second_ref)[j // per][i * per + j % per], states[j]) for j in range(heads)]
 
 
 def spread(start, first, second):
     heads, size, _ = start.shape
+    members = 2 * first.shape[0] // heads
     return pl.pallas_call(
         spread_kernel,
-        out_shape=jax.ShapeDtypeStruct((first.shape[0], heads, size, size), F32),
+        in_specs=[IN_VMEM] * 3,
+        out_specs=IN_VMEM,
+        out_shape=jax.ShapeDtypeStruct((members * heads, size, size), F32),
         compiler_params=pltpu.CompilerParams(vmem_limit_bytes=VMEM),
         name="spread",
     )(start, first, second)
 
 
-def finish_kernel(lout_ref, cq_ref, state_ref, gain_ref, out_ref):
-    for h in range(lout_ref.shape[0]):
-        outs = lout_ref[h] + mm3(left3(cq_ref[h]), right3(state_ref[h]))
-        total = jnp.mean(outs * outs, axis=1, keepdims=True) + EPS
-        normed = outs / jnp.sqrt(total) * gain_ref[:, head_cols(h)]
-        out_ref[:, head_cols(h)] = normed.astype(BF16)
+def finish_kernel(lout_ref, cq_ref, states, gain_ref, out_ref):
+    rights = [right3(state) for state in states]
+    outs = [lout_ref[h] + mm3(left3(cq_ref[h]), right) for h, right in enumerate(rights)]
+    roots = [jnp.sqrt(jnp.mean(out * out, axis=1, keepdims=True) + EPS) for out in outs]
+    for h, (out, root) in enumerate(zip(outs, roots)):
+        out_ref[:, head_cols(h)] = (out / root * gain_ref[:, head_cols(h)]).astype(BF16)
 
 
 def finish(tokens, state, gain):
     (lout0, cq0), (lout1, cq1) = tokens
     count, size = lout0.shape[1], lout0.shape[2]
-    members, groups, per = state.shape[0], state.shape[1], state.shape[2]
-    heads = members * groups * per
+    groups, heads = 2, state.shape[0]
+    per = 2
+    step_heads = 4
+    steps = heads // step_heads
+    half = steps // groups
 
     def kernel(l0, c0, l1, c1, state_ref, gain_ref, out_ref):
-        pick = pl.program_id(0) < members
-
-        @pl.when(pick)
+        at = pl.program_id(0)
+
+        def run(lout_ref, cq_ref, group):
+            first = (at - group * half) * (step_heads // per)
+            states = [state_ref[(first + h // per) * groups * per + group * per + h % per] for h in range(step_heads)]
+            finish_kernel(lout_ref, cq_ref, states, gain_ref, out_ref)
+
+        @pl.when(at < half)
         def _():
-            finish_kernel(l0, c0, state_ref, gain_ref, out_ref)
-
-        @pl.when(jnp.logical_not(pick))
+            run(l0, c0, 0)
+
+        @pl.when(at >= half)
         def _():
-            finish_kernel(l1, c1, state_ref, gain_ref, out_ref)
-
-    low = pl.BlockSpec((per, count, size), lambda g: (jnp.minimum(g, members - 1), 0, 0))
-    high = pl.BlockSpec((per, count, size), lambda g: (jnp.maximum(g - members, 0), 0, 0))
+            run(l1, c1, 1)
+
+    low = pl.BlockSpec((step_heads, count, size), lambda g: (jnp.minimum(g, half - 1), 0, 0))
+    high = pl.BlockSpec((step_heads, count, size), lambda g: (jnp.maximum(g - half, 0), 0, 0))
     return pl.pallas_call(
         kernel,
-        grid=(members * groups,),
+        grid=(steps,),
         in_specs=[
             low,
             low,
             high,
             high,
-            pl.BlockSpec((None, None, per, size, size), lambda g: (g % members, g // members, 0, 0, 0)),
-            pl.BlockSpec((1, per * size), lambda g: (0, g)),
-        ],
-        out_specs=pl.BlockSpec((count, per * size), lambda g: (0, g)),
+            IN_VMEM,
+            pl.BlockSpec((1, step_heads * size), lambda g: (0, g)),
+        ],
+        out_specs=pl.BlockSpec((count, step_heads * size), lambda g: (0, g)),
         out_shape=jax.ShapeDtypeStruct((count, heads * size), BF16),
         compiler_params=pltpu.CompilerParams(vmem_limit_bytes=VMEM),
         name="finish",
@@ -365,31 +425,26 @@
 
 
 def local(queries, keys, values, beta_logit, gain):
-    count, width = queries.shape
-    keys = keys.reshape(2 * count, width)
-    values = values.reshape(2 * count, width)
     quad = lax.axis_size("zi")
-    size = 128
     received = []
     saved = []
     for group in range(2):
         maps, inv, cross, scale = block_maps(group, keys, values, beta_logit)
         saved.append((inv, cross, scale))
         got = lax.all_to_all(maps, "zi", split_axis=0, concat_axis=0, tiled=True)
-        received.append(got.reshape(quad, GROUP // quad, size, 2 * size))
+        received.append(got)
     tokens = [block_tokens(group, queries, keys, values, *saved[group]) for group in range(2)]
-    totals = jnp.concatenate([chain(got, "quad_total") for got in received], axis=0)
+    totals = chain("quad_total", quad, received[1], chain("quad_total", quad, received[0]))
     quads = lax.all_to_all(totals, "zq", split_axis=0, concat_axis=0, tiled=True)
-    whole = chain(quads[:, None], "group_total")
+    whole = chain("group_total", lax.axis_size("zq"), quads)
     by_core = lax.all_gather(whole[0], "core")
-    by_y = lax.all_gather(chain(by_core[:, None], "chip_total")[0], "y")
-    by_x = lax.all_gather(chain(by_y[:, None], "y_total")[0], "x")
+    by_y = lax.all_gather(chain("chip_total", lax.axis_size("core"), by_core)[0], "y")
+    by_x = lax.all_gather(chain("y_total", lax.axis_size("y"), by_y)[0], "x")
     place = jnp.stack([lax.axis_index("x"), lax.axis_index("y"), lax.axis_index("core")])
     starts = start_states(place, by_x, by_y, by_core, quads)
     mine = lax.all_to_all(starts, "zq", split_axis=0, concat_axis=0, tiled=True)
     entries = spread(mine, received[0], received[1])
     state = lax.all_to_all(entries, "zi", split_axis=0, concat_axis=0, tiled=True)
-    state = state.reshape(quad, 2, GROUP // quad, size, size)
     return finish(tokens, state, gain)
 
 

time: 234 us -> 214 us (0.915)
  Pallas kernels: 83.3 us -> 57.4 us
  waiting for transfers between devices: 61.7 us -> 72.5 us
  local copies, waits for them, and re-layouts: 7.35 us -> 3.74 us
    pallas_call x9, Pallas kernels: 65.5 us -> 38.7 us  [the longest x2 19 us: block_maps(): pl.pallas_call(maps_kernel, grid=(1,), in_specs=[pl.BlockSpec((rows // 2,...]
    all_to_all x2, waiting for transfers between devices: 26.7 us -> 38.8 us  [local(): got = lax.all_to_all(maps, 'zi', split_axis=0, concat_axis=0, tiled=True)]
    reshape x2 -> x0, local copies, waits for them, and re-layouts: 3.57 us -> none  [the longest x1 2.34 us: local(): keys = keys.reshape(2 * count, width)]
  transfers between devices with their start and end apart: 4 -> 4, of which waited for: 4 -> 4; matrix products, arithmetic and copies ran while one was open for 0% -> 0% of each run, Pallas kernels for 17% -> 13%
where the time goes in v2:
time: 214 us; the launch traced here: 212 us
  waiting for transfers between devices  72.5 us (34%)
  Pallas kernels  57.4 us (27%)
  blocking collectives  52.1 us (24%)
  starting transfers between devices  26.1 us (12%)
  local copies, waits for them, and re-layouts  3.74 us (2%)
    all_to_all x2, waiting for transfers between devices, local(): got = lax.all_to_all(maps, 'zi', split_axis=0, concat_axis=0, tiled=True)  38.8 us
    all_to_all x1, waiting for transfers between devices, local(): lax.all_to_all(totals, 'zq', split_axis=0, concat_axis=0, tiled=True)  28.6 us
    pallas_call x2, Pallas kernels, block_maps(): pl.pallas_call(maps_kernel, grid=(1,), in_specs=[pl.BlockSpec((rows // 2,...  19 us
    all_to_all x1, blocking collectives, local(): mine = lax.all_to_all(starts, 'zq', split_axis=0, concat_axis=0, tiled=True)  18.9 us
    pallas_call x2, Pallas kernels, block_tokens(): pl.pallas_call(tokens_kernel, grid=(1,), in_specs=[pl.BlockSpec((count, l...  15.5 us
    all_gather x1, blocking collectives, local(): lax.all_gather(chain('chip_total', lax.axis_size('core'), by_core)[0], 'y')  15.4 us
    all_gather x1, blocking collectives, local(): by_x = lax.all_gather(chain('y_total', lax.axis_size('y'), by_y)[0], 'x')  14.4 us
    all_to_all x1, starting transfers between devices, local(): lax.all_to_all(totals, 'zq', split_axis=0, concat_axis=0, tiled=True)  13 us
  transfers between devices with their start and end apart: 4, of which 4 were waited for; matrix products, arithmetic and copies ran while one was open for 0% of the time, Pallas kernels for 13%

profile of v2, /device:TPU:6, one launch (start us, length us, event | category | flops | bytes accessed | tf_op | source)
XLA Modules:
  0.0 212.5 jit_solution(7580148406710561298)
XLA Ops:
  0.0 9.5 %block_maps.2 = (f32[8,128,256]{2,1,0:T(8,128)}, f32[8,256,128]{2,1,0:T(8,128)}, f32[8,128,128]{2,1,0:T(8,128)}, f32[8,256]{1,0:T(8,128)}) custom-call(bf16[128,2,2048]{2,1,0:T(2,128)(2,1)} %k_ref.7, bf16[128,2,2048]{2,1,0:T(2,128)(2,1)} %v_ref.7, f32[2,16,128]{2,1,0:T(8,128)} %logit_ref.3), custom_call_target="tpu_custom_call" | custom-call | tf_op jit(solution)/shard_map/block_maps/pallas_call | solution.py:210
  9.5 5.9 %all-to-all-start.1 = ((f32[8,128,256]{2,1,0:T(8,128)}), f32[8,128,256]{2,1,0:T(8,128)S(1)}, u32[]{:S(2)}, u32[]{:S(2)}) async-start(f32[8,128,256]{2,1,0:T(8,128)} %get-tuple-element.28), calls=%async_computation.1 | async-start | bytes 2097152 | tf_op jit(solution)/shard_map/all_to_all | solution.py:434
  15.4 9.5 %block_maps.3 = (f32[8,128,256]{2,1,0:T(8,128)}, f32[8,256,128]{2,1,0:T(8,128)}, f32[8,128,128]{2,1,0:T(8,128)}, f32[8,256]{1,0:T(8,128)}) custom-call(bf16[128,2,2048]{2,1,0:T(2,128)(2,1)} %k_ref.7, bf16[128,2,2048]{2,1,0:T(2,128)(2,1)} %v_ref.7, f32[2,16,128]{2,1,0:T(8,128)} %logit_ref.3), custom_call_target="tpu_custom_call" | custom-call | tf_op jit(solution)/shard_map/block_maps/pallas_call | solution.py:210
  24.9 16.2 %all-to-all-done.1.maps_ref.first_ref = f32[8,128,256]{2,1,0:T(8,128)S(1)} async-done(((f32[8,128,256]{2,1,0:T(8,128)}), f32[8,128,256]{2,1,0:T(8,128)S(1)}, u32[]{:S(2)}, u32[]{:S(2)}) %all-to-all-start.1) | async-done | bytes 1048608 | tf_op jit(solution)/shard_map/all_to_all | solution.py:434
  41.1 0.0 copy-start
  41.1 1.0 copy-done
  42.1 3.5 %all-to-all-start = ((f32[8,128,256]{2,1,0:T(8,128)}), f32[8,128,256]{2,1,0:T(8,128)S(1)}, u32[]{:S(2)}, u32[]{:S(2)}) async-start(f32[8,128,256]{2,1,0:T(8,128)} %get-tuple-element.27), calls=%async_computation | async-start | bytes 2097152 | tf_op jit(solution)/shard_map/all_to_all | solution.py:434
  45.6 2.6 %quad_total.2.refs_0_ = f32[2,128,256]{2,1,0:T(8,128)} custom-call(f32[8,128,256]{2,1,0:T(8,128)} %copy-done), custom_call_target="tpu_custom_call" | custom-call | tf_op jit(solution)/shard_map/quad_total/pallas_call | solution.py:316
  48.2 22.6 %all-to-all-done.maps_ref.second_ref = f32[8,128,256]{2,1,0:T(8,128)S(1)} async-done(((f32[8,128,256]{2,1,0:T(8,128)}), f32[8,128,256]{2,1,0:T(8,128)S(1)}, u32[]{:S(2)}, u32[]{:S(2)}) %all-to-all-start) | async-done | bytes 1048608 | tf_op jit(solution)/shard_map/all_to_all | solution.py:434
  70.8 0.0 copy-start.1
  70.8 1.0 copy-done.1
  71.8 2.7 %quad_total.3 = f32[4,128,256]{2,1,0:T(8,128)} custom-call(f32[8,128,256]{2,1,0:T(8,128)} %copy-done.1, f32[2,128,256]{2,1,0:T(8,128)} %quad_total.2.refs_0_), custom_call_target="tpu_custom_call" | custom-call | tf_op jit(solution)/shard_map/quad_total/pallas_call | solution.py:316
  74.5 13.0 %all-to-all-start.2 = ((f32[4,128,256]{2,1,0:T(8,128)}), f32[4,128,256]{2,1,0:T(8,128)S(1)}, u32[]{:S(2)}, u32[]{:S(2)}) async-start(f32[4,128,256]{2,1,0:T(8,128)} %quad_total.3), calls=%async_computation.2 | async-start | bytes 1048576 | tf_op jit(solution)/shard_map/all_to_all | solution.py:438
  87.5 0.6 pad_add_fusion.place_ref
  88.1 28.6 %all-to-all-done.2.maps_ref.quads_ref = f32[4,128,256]{2,1,0:T(8,128)S(1)} async-done(((f32[4,128,256]{2,1,0:T(8,128)}), f32[4,128,256]{2,1,0:T(8,128)S(1)}, u32[]{:S(2)}, u32[]{:S(2)}) %all-to-all-start.2) | async-done | bytes 524320 | tf_op jit(solution)/shard_map/all_to_all | solution.py:438
  116.7 0.0 copy-start.2
  116.7 0.8 copy-done.2
  117.5 2.3 %group_total.1 = f32[1,128,256]{2,1,0:T(8,128)} custom-call(f32[4,128,256]{2,1,0:T(8,128)} %copy-done.2), custom_call_target="tpu_custom_call" | custom-call | tf_op jit(solution)/shard_map/group_total/pallas_call | solution.py:316
  119.8 3.5 %all_gather.9.maps_ref.by_core_ref = f32[2,128,256]{2,1,0:T(8,128)} all-gather(f32[1,128,256]{2,1,0:T(8,128)} %group_total.1), channel_id=1, replica_groups=mesh['x'=4,'y'=4,'core'=2,'zq'=4,'zi'=4] {'core'}, dimensions={0}, use_global_device_ids=true | all-gather | bytes 393216 | tf_op jit(solution)/shard_map/all_gather | solution.py:440
  123.2 1.8 chip_total.1
  125.0 15.4 %all_gather.10.maps_ref.by_y_ref = f32[4,128,256]{2,1,0:T(8,128)} all-gather(f32[1,128,256]{2,1,0:T(8,128)} %chip_total.1), channel_id=1, replica_groups=mesh['x'=4,'y'=4,'core'=2,'zq'=4,'zi'=4] {'y'}, dimensions={0}, use_global_device_ids=true | all-gather | bytes 655360 | tf_op jit(solution)/shard_map/all_gather | solution.py:441
  140.4 2.3 %y_total.1 = f32[1,128,256]{2,1,0:T(8,128)} custom-call(f32[4,128,256]{2,1,0:T(8,128)} %all_gather.10.maps_ref.by_y_ref), custom_call_target="tpu_custom_call" | custom-call | tf_op jit(solution)/shard_map/y_total/pallas_call | solution.py:316
  142.6 14.4 %all_gather.11.by_x_ref = f32[4,128,256]{2,1,0:T(8,128)} all-gather(f32[1,128,256]{2,1,0:T(8,128)} %y_total.1), channel_id=1, replica_groups=mesh['x'=4,'y'=4,'core'=2,'zq'=4,'zi'=4] {'x'}, dimensions={0}, use_global_device_ids=true | all-gather | bytes 655360 | tf_op jit(solution)/shard_map/all_gather | solution.py:442
  157.0 3.2 %start_states.1 = f32[4,128,128]{2,1,0:T(8,128)} custom-call(s32[3]{0:T(128)} %pad_add_fusion.place_ref, f32[4,128,256]{2,1,0:T(8,128)} %all_gather.11.by_x_ref, f32[4,128,256]{2,1,0:T(8,128)} %all_gather.10.maps_ref.by_y_ref, f32[2,128,256]{2,1,0:T(8,128)} %all_gather.9.maps_ref.by_core_ref, f32[4,128,256]{2,1,0:T(8,128)} %copy-done.2), custom_call_target="tpu_custom_call" | custom-call | tf_op jit(solution)/shard_map/start_states/pallas_call | solution.py:339
  160.3 18.9 %all_to_all.25.start_ref = f32[4,128,128]{2,1,0:T(8,128)} all-to-all(f32[4,128,128]{2,1,0:T(8,128)} %start_states.1), channel_id=1, replica_groups=mesh['x'=4,'y'=4,'core'=2,'zq'=4,'zi'=4] {'zq'}, dimensions={0} | all-to-all | bytes 524288 | tf_op jit(solution)/shard_map/all_to_all | solution.py:445
  179.1 3.2 %spread.1 = f32[16,128,128]{2,1,0:T(8,128)} custom-call(f32[4,128,128]{2,1,0:T(8,128)} %all_to_all.25.start_ref, f32[8,128,256]{2,1,0:T(8,128)} %copy-done, f32[8,128,256]{2,1,0:T(8,128)} %copy-done.1), custom_call_target="tpu_custom_call" | custom-call | tf_op jit(solution)/shard_map/spread/pallas_call | solution.py:364
  182.4 3.7 %all-to-all-start.4 = ((f32[16,128,128]{2,1,0:T(8,128)}), f32[16,128,128]{2,1,0:T(8,128)S(1)}, u32[]{:S(2)}, u32[]{:S(2)}) async-start(f32[16,128,128]{2,1,0:T(8,128)} %spread.1), calls=%async_computation.4 | async-start | bytes 2097152 | tf_op jit(solution)/shard_map/all_to_all | solution.py:447
  186.1 7.8 %block_tokens.3 = (f32[8,128,128]{2,1,0:T(8,128)}, f32[8,128,128]{2,1,0:T(8,128)}) custom-call(bf16[128,2048]{1,0:T(8,128)(2,1)} %q_ref.3, bf16[128,2,2048]{2,1,0:T(2,128)(2,1)} %k_ref.7, bf16[128,2,2048]{2,1,0:T(2,128)(2,1)} %v_ref.7, f32[8,256,128]{2,1,0:T(8,128)} %get-tuple-element.22.inv_ref, f32[8,128,128]{2,1,0:T(8,128)} %get-tuple-element.23.cross_ref, ...), custom_call_target="tpu_custom_call" | custom-call | tf_op jit(solution)/shard_map/block_tokens/pallas_call | solution.py:263
  193.9 7.8 %block_tokens.2 = (f32[8,128,128]{2,1,0:T(8,128)}, f32[8,128,128]{2,1,0:T(8,128)}) custom-call(bf16[128,2048]{1,0:T(8,128)(2,1)} %q_ref.3, bf16[128,2,2048]{2,1,0:T(2,128)(2,1)} %k_ref.7, bf16[128,2,2048]{2,1,0:T(2,128)(2,1)} %v_ref.7, f32[8,256,128]{2,1,0:T(8,128)} %get-tuple-element.17.inv_ref, f32[8,128,128]{2,1,0:T(8,128)} %get-tuple-element.18.cross_ref, ...), custom_call_target="tpu_custom_call" | custom-call | tf_op jit(solution)/shard_map/block_tokens/pallas_call | solution.py:263
  201.7 5.0 %all-to-all-done.4.state_ref = f32[16,128,128]{2,1,0:T(8,128)S(1)} async-done(((f32[16,128,128]{2,1,0:T(8,128)}), f32[16,128,128]{2,1,0:T(8,128)S(1)}, u32[]{:S(2)}, u32[]{:S(2)}) %all-to-all-start.4) | async-done | bytes 1048608 | tf_op jit(solution)/shard_map/all_to_all | solution.py:447
  206.7 0.0 copy-start.3
  206.7 1.0 copy-done.3
  207.7 4.8 %finish.1 = bf16[128,2048]{1,0:T(8,128)(2,1)} custom-call(f32[8,128,128]{2,1,0:T(8,128)} %get-tuple-element.20.l0, f32[8,128,128]{2,1,0:T(8,128)} %get-tuple-element.21.c0, f32[8,128,128]{2,1,0:T(8,128)} %get-tuple-element.25.l1, f32[8,128,128]{2,1,0:T(8,128)} %get-tuple-element.26.c1, f32[16,128,128]{2,1,0:T(8,128)} %copy-done.3, f32[1,2048]{1,0:T(1,128)} %bitcast.4), custom_call_target="tpu_custom_call" | custom-call | tf_op jit(solution)/shard_map/finish/pallas_call | solution.py:409
Async XLA Ops:
  9.5 31.6 %all-to-all-start.1 = ((f32[8,128,256]{2,1,0:T(8,128)}), f32[8,128,256]{2,1,0:T(8,128)S(1)}, u32[]{:S(2)}, u32[]{:S(2)}) async-start(f32[8,128,256]{2,1,0:T(8,128)} %get-tuple-element.28), calls=%async_computation.1 | async-start | bytes 2097152 | tf_op jit(solution)/shard_map/all_to_all | solution.py:434
  41.1 1.0 copy-start
  42.1 28.7 %all-to-all-start = ((f32[8,128,256]{2,1,0:T(8,128)}), f32[8,128,256]{2,1,0:T(8,128)S(1)}, u32[]{:S(2)}, u32[]{:S(2)}) async-start(f32[8,128,256]{2,1,0:T(8,128)} %get-tuple-element.27), calls=%async_computation | async-start | bytes 2097152 | tf_op jit(solution)/shard_map/all_to_all | solution.py:434
  70.8 1.0 copy-start.1
  74.5 42.2 %all-to-all-start.2 = ((f32[4,128,256]{2,1,0:T(8,128)}), f32[4,128,256]{2,1,0:T(8,128)S(1)}, u32[]{:S(2)}, u32[]{:S(2)}) async-start(f32[4,128,256]{2,1,0:T(8,128)} %quad_total.3), calls=%async_computation.2 | async-start | bytes 1048576 | tf_op jit(solution)/shard_map/all_to_all | solution.py:438
  116.7 0.8 copy-start.2
  182.4 24.3 %all-to-all-start.4 = ((f32[16,128,128]{2,1,0:T(8,128)}), f32[16,128,128]{2,1,0:T(8,128)S(1)}, u32[]{:S(2)}, u32[]{:S(2)}) async-start(f32[16,128,128]{2,1,0:T(8,128)} %spread.1), calls=%async_computation.4 | async-start | bytes 2097152 | tf_op jit(solution)/shard_map/all_to_all | solution.py:447
  206.7 1.0 copy-start.3

commit v3 on v2

--- a/solution.py
+++ b/solution.py
@@ -11,6 +11,7 @@
 BF16 = jnp.bfloat16
 BASE = 16
 GROUP = 128 // BASE
+CHUNKS = ((0, 4), (4, 12))
 EPS = 1e-06
 VMEM = 56 * 1024 * 1024
 
@@ -101,7 +102,7 @@
     return prod[:, :128] + dot(z_hi, k_lo), prod[:, 128:]
 
 
-def maps_kernel(k_ref, v_ref, logit_ref, maps_ref, inv_ref, cross_ref, scale_ref, n_ref, r_ref, c_ref, t_ref, z_ref):
+def maps_kernel(first, heads, skip, k_ref, v_ref, logit_ref, maps_ref, inv_ref, cross_ref, scale_ref, n_ref, r_ref, c_ref, t_ref, z_ref):
     rows = 2 * k_ref.shape[0]
     size = 128
     beta_rows = beta_rows_of(logit_ref[...])
@@ -114,33 +115,36 @@
     col128 = iota((size, size), 1)
     eye_b = (row128 == col128).astype(BF16)
 
-    compact = [jnp.zeros((BASE, 128), F32) for _ in range(rows // BASE)]
+    packs = -(-heads // GROUP)
+    compact = [jnp.zeros((BASE, 128), F32) for _ in range(packs * (rows // BASE))]
     lane = iota((BASE, 128), 1)
-    for h in range(GROUP):
-        kb = head_rows(k_ref, h)
+    for h in range(heads):
+        kb = head_rows(k_ref, skip + h)
         grams = dot_nt(jnp.concatenate([kb, eye_b], axis=0), kb)
         gram = grams[:rows]
         kf = kb.astype(F32)
         n_col = reciprocal_root(jnp.sum(kf * kf, axis=1, keepdims=True) + EPS)
         n_row = reciprocal_root(jnp.sum(jnp.where(diagonal, gram, 0.0), axis=0, keepdims=True) + EPS)
-        scale_row = n_row * beta_rows[h : h + 1, :]
+        scale_row = n_row * beta_rows[first + h : first + h + 1, :]
         scale_ref[h : h + 1, :] = scale_row
         system = jnp.where(strict, gram, 0.0) * n_col * scale_row
         n_ref[h] = system
         cross_ref[h] = system[size:, :size]
         r_ref[h] = grams[rows:] * scale_row
-        mine = (lane // BASE) == h
+        slot = h % GROUP
+        mine = (lane // BASE) == slot
         for blk in range(rows // BASE):
             place = blk % GROUP
             tile = blk // GROUP
             slab = system[blk * BASE : (blk + 1) * BASE, tile * 128 : (tile + 1) * 128]
-            shift = BASE * ((h - place) % GROUP)
+            shift = BASE * ((slot - place) % GROUP)
             if shift:
                 slab = pltpu.roll(slab, shift, axis=1)
-            compact[blk] = jnp.where(mine, slab, compact[blk])
+            at = (h // GROUP) * (rows // BASE) + blk
+            compact[at] = jnp.where(mine, slab, compact[at])
 
     identity = (iota((BASE, 128), 0) == (lane % BASE)).astype(F32)
-    for blk in range(rows // BASE):
+    for blk in range(packs * (rows // BASE)):
         below = compact[blk]
         inv = identity
         for step in range(BASE - 1):
@@ -148,11 +152,11 @@
             inv = inv - factor * inv[step : step + 1, :]
         c_ref[blk] = inv
 
-    for h in range(GROUP):
+    for h in range(heads):
         for tile in range(2):
             for place in range(GROUP):
-                slab = c_ref[tile * GROUP + place]
-                shift = BASE * ((place - h) % GROUP)
+                slab = c_ref[(h // GROUP) * (rows // BASE) + tile * GROUP + place]
+                shift = BASE * ((place - h % GROUP) % GROUP)
                 if shift:
                     slab = pltpu.roll(slab, shift, axis=1)
                 first = tile * 128 + place * BASE
@@ -161,7 +165,7 @@
     while width < size:
         odd = range(width, size, 2 * width)
         mask = col128[:width] // width
-        for h in range(GROUP):
+        for h in range(heads):
             for tile in range(2):
                 base = tile * 128
                 inv = inv_ref[h, base : base + 128]
@@ -173,7 +177,7 @@
                     axis=0,
                 )
                 t_ref[h, tile] = mm3(left3(part), right3(inv))
-        for h in range(GROUP):
+        for h in range(heads):
             for tile in range(2):
                 base = tile * 128
                 own = jnp.concatenate([inv_ref[h, base + at : base + at + width] for at in odd], axis=0)
@@ -190,91 +194,95 @@
         width *= 2
 
     eye = (row128 == col128).astype(F32)
-    for h in range(GROUP):
+    for h in range(heads):
         z_ref[h, :, size:] = mm3(left3(r_ref[h, :, size:]), right3(inv_ref[h, size:]))
-    for h in range(GROUP):
+    for h in range(heads):
         r_ref[h, :, :size] = r_ref[h, :, :size] - mm3(left3(z_ref[h, :, size:]), right3(cross_ref[h]))
-    for h in range(GROUP):
+    for h in range(heads):
         z_ref[h, :, :size] = mm3(left3(r_ref[h, :, :size]), right3(inv_ref[h, :size]))
-    for h in range(GROUP):
-        through, fresh = through_rows(z_ref[h], head_rows(k_ref, h), head_rows(v_ref, h))
+    for h in range(heads):
+        through, fresh = through_rows(z_ref[h], head_rows(k_ref, skip + h), head_rows(v_ref, skip + h))
         maps_ref[h, :, :size] = eye - through
         maps_ref[h, :, size:] = fresh
 
 
-def block_maps(group, keys, values, logits):
+def whole(*shape):
+    return pl.BlockSpec(shape, lambda g: (0,) * len(shape))
+
+
+def block_maps(chunk, keys, values, logits):
+    first, heads = chunk
     rows = 2 * keys.shape[0]
     size = 128
-    lanes = GROUP * size
-    whole = lambda *shape: pl.BlockSpec(shape, lambda g: (0,) * len(shape))
-    return pl.pallas_call(
-        maps_kernel,
+    lanes = heads * size if first == 0 else keys.shape[2]
+    return pl.pallas_call(
+        functools.partial(maps_kernel, first, heads, first),
         grid=(1,),
         in_specs=[
-            pl.BlockSpec((rows // 2, 2, lanes), lambda g: (0, 0, group)),
-            pl.BlockSpec((rows // 2, 2, lanes), lambda g: (0, 0, group)),
-            pl.BlockSpec((2, GROUP, rows // 2), lambda g: (0, group, 0)),
+            whole(rows // 2, 2, lanes),
+            whole(rows // 2, 2, lanes),
+            whole(*logits.shape),
         ],
         out_specs=[
-            whole(GROUP, size, 2 * size),
-            whole(GROUP, rows, size),
-            whole(GROUP, size, size),
-            whole(GROUP, rows),
+            whole(heads, size, 2 * size),
+            whole(heads, rows, size),
+            whole(heads, size, size),
+            whole(heads, rows),
         ],
         out_shape=[
-            jax.ShapeDtypeStruct((GROUP, size, 2 * size), F32),
-            jax.ShapeDtypeStruct((GROUP, rows, size), F32),
-            jax.ShapeDtypeStruct((GROUP, size, size), F32),
-            jax.ShapeDtypeStruct((GROUP, rows), F32),
+            jax.ShapeDtypeStruct((heads, size, 2 * size), F32),
+            jax.ShapeDtypeStruct((heads, rows, size), F32),
+            jax.ShapeDtypeStruct((heads, size, size), F32),
+            jax.ShapeDtypeStruct((heads, rows), F32),
         ],
         scratch_shapes=[
-            pltpu.VMEM((GROUP, rows, rows), F32),
-            pltpu.VMEM((GROUP, size, rows), F32),
-            pltpu.VMEM((rows // BASE, BASE, 128), F32),
-            pltpu.VMEM((GROUP, 2, size // 2, size), F32),
-            pltpu.VMEM((GROUP, size, rows), F32),
+            pltpu.VMEM((heads, rows, rows), F32),
+            pltpu.VMEM((heads, size, rows), F32),
+            pltpu.VMEM((-(-heads // GROUP) * (rows // BASE), BASE, 128), F32),
+            pltpu.VMEM((heads, 2, size // 2, size), F32),
+            pltpu.VMEM((heads, size, rows), F32),
         ],
         compiler_params=pltpu.CompilerParams(vmem_limit_bytes=VMEM),
         name="block_maps",
     )(keys, values, logits)
 
 
-def tokens_kernel(q_ref, k_ref, v_ref, inv_ref, cross_ref, scale_ref, lout_ref, cq_ref):
+def tokens_kernel(skip, q_ref, k_ref, v_ref, inv_ref, cross_ref, scale_ref, lout_ref, cq_ref):
     count = q_ref.shape[0]
     seen = iota((count, 2 * count), 1) <= 2 * iota((count, 2 * count), 0) + 1
-    for h in range(GROUP):
-        kb = head_rows(k_ref, h)
-        qb = q_ref[:, head_cols(h)]
+    for h in range(lout_ref.shape[0]):
+        kb = head_rows(k_ref, skip + h)
+        qb = q_ref[:, head_cols(skip + h)]
         scores = jnp.where(seen, dot_nt(qb, kb), 0.0) * scale_ref[h : h + 1, :]
         z = solve_right(scores, inv_ref[h], cross_ref[h])
-        through, fresh = through_rows(z, kb, head_rows(v_ref, h))
+        through, fresh = through_rows(z, kb, head_rows(v_ref, skip + h))
         qf = qb.astype(F32)
         nq = reciprocal_root(jnp.sum(qf * qf, axis=1, keepdims=True) + EPS)
         cq_ref[h] = nq * (qf - through)
         lout_ref[h] = nq * fresh
 
 
-def block_tokens(group, queries, keys, values, inv, cross, scale):
-    count, width = queries.shape
+def block_tokens(chunk, queries, keys, values, inv, cross, scale):
+    first, heads = chunk
+    count = queries.shape[0]
     rows = 2 * count
     size = 128
-    lanes = GROUP * size
-    whole = lambda *shape: pl.BlockSpec(shape, lambda g: (0,) * len(shape))
-    return pl.pallas_call(
-        tokens_kernel,
+    lanes = heads * size if first == 0 else queries.shape[1]
+    return pl.pallas_call(
+        functools.partial(tokens_kernel, first),
         grid=(1,),
         in_specs=[
-            pl.BlockSpec((count, lanes), lambda g: (0, group)),
-            pl.BlockSpec((rows // 2, 2, lanes), lambda g: (0, 0, group)),
-            pl.BlockSpec((rows // 2, 2, lanes), lambda g: (0, 0, group)),
-            whole(GROUP, rows, size),
-            whole(GROUP, size, size),
-            whole(GROUP, rows),
-        ],
-        out_specs=[whole(GROUP, count, size), whole(GROUP, count, size)],
+            whole(count, lanes),
+            whole(rows // 2, 2, lanes),
+            whole(rows // 2, 2, lanes),
+            whole(heads, rows, size),
+            whole(heads, size, size),
+            whole(heads, rows),
+        ],
+        out_specs=[whole(heads, count, size), whole(heads, count, size)],
         out_shape=[
-            jax.ShapeDtypeStruct((GROUP, count, size), F32),
-            jax.ShapeDtypeStruct((GROUP, count, size), F32),
+            jax.ShapeDtypeStruct((heads, count, size), F32),
+            jax.ShapeDtypeStruct((heads, count, size), F32),
         ],
         compiler_params=pltpu.CompilerParams(vmem_limit_bytes=VMEM),
         name="block_tokens",
@@ -348,19 +356,21 @@
 
 def spread_kernel(start_ref, first_ref, second_ref, entry_ref):
     heads = start_ref.shape[0]
-    per = heads // 2
-    members = first_ref.shape[0] // per
+    members = entry_ref.shape[0] // heads
+    early = first_ref.shape[0] // members
+    late = heads - early
     states = [start_ref[j] for j in range(heads)]
     for i in range(members):
         for j in range(heads):
             entry_ref[i * heads + j] = states[j]
         if i < members - 1:
-            states = [advance((first_ref, second_ref)[j // per][i * per + j % per], states[j]) for j in range(heads)]
+            pieces = [first_ref[i * early + j] for j in range(early)] + [second_ref[i * late + j] for j in range(late)]
+            states = [advance(piece, state) for piece, state in zip(pieces, states)]
 
 
 def spread(start, first, second):
     heads, size, _ = start.shape
-    members = 2 * first.shape[0] // heads
+    members = (first.shape[0] + second.shape[0]) // heads
     return pl.pallas_call(
         spread_kernel,
         in_specs=[IN_VMEM] * 3,
@@ -382,42 +392,35 @@
 def finish(tokens, state, gain):
     (lout0, cq0), (lout1, cq1) = tokens
     count, size = lout0.shape[1], lout0.shape[2]
-    groups, heads = 2, state.shape[0]
-    per = 2
-    step_heads = 4
-    steps = heads // step_heads
-    half = steps // groups
+    heads = state.shape[0]
+    early = lout0.shape[0]
+    held = heads // early
+    late = held - 1
 
     def kernel(l0, c0, l1, c1, state_ref, gain_ref, out_ref):
         at = pl.program_id(0)
 
-        def run(lout_ref, cq_ref, group):
-            first = (at - group * half) * (step_heads // per)
-            states = [state_ref[(first + h // per) * groups * per + group * per + h % per] for h in range(step_heads)]
-            finish_kernel(lout_ref, cq_ref, states, gain_ref, out_ref)
-
-        @pl.when(at < half)
+        @pl.when(at == 0)
         def _():
-            run(l0, c0, 0)
-
-        @pl.when(at >= half)
+            states = [state_ref[held * m] for m in range(early)]
+            finish_kernel(l0, c0, states, gain_ref, out_ref)
+
+        @pl.when(at > 0)
         def _():
-            run(l1, c1, 1)
-
-    low = pl.BlockSpec((step_heads, count, size), lambda g: (jnp.minimum(g, half - 1), 0, 0))
-    high = pl.BlockSpec((step_heads, count, size), lambda g: (jnp.maximum(g - half, 0), 0, 0))
+            states = []
+            for h in range(early):
+                place = (at - 1) * early + h
+                member = lax.div(place, late)
+                states.append(state_ref[held * member + 1 + place - late * member])
+            finish_kernel(l1, c1, states, gain_ref, out_ref)
+
+    low = pl.BlockSpec((early, count, size), lambda g: (0, 0, 0))
+    high = pl.BlockSpec((early, count, size), lambda g: (jnp.maximum(g - 1, 0), 0, 0))
     return pl.pallas_call(
         kernel,
-        grid=(steps,),
-        in_specs=[
-            low,
-            low,
-            high,
-            high,
-            IN_VMEM,
-            pl.BlockSpec((1, step_heads * size), lambda g: (0, g)),
-        ],
-        out_specs=pl.BlockSpec((count, step_heads * size), lambda g: (0, g)),
+        grid=(heads // early,),
+        in_specs=[low, low, high, high, IN_VMEM, pl.BlockSpec((1, early * size), lambda g: (0, g))],
+        out_specs=pl.BlockSpec((count, early * size), lambda g: (0, g)),
         out_shape=jax.ShapeDtypeStruct((count, heads * size), BF16),
         compiler_params=pltpu.CompilerParams(vmem_limit_bytes=VMEM),
         name="finish",
@@ -428,12 +431,12 @@
     quad = lax.axis_size("zi")
     received = []
     saved = []
-    for group in range(2):
-        maps, inv, cross, scale = block_maps(group, keys, values, beta_logit)
+    for chunk in CHUNKS:
+        maps, inv, cross, scale = block_maps(chunk, keys, values, beta_logit)
         saved.append((inv, cross, scale))
         got = lax.all_to_all(maps, "zi", split_axis=0, concat_axis=0, tiled=True)
         received.append(got)
-    tokens = [block_tokens(group, queries, keys, values, *saved[group]) for group in range(2)]
+    tokens = [block_tokens(chunk, queries, keys, values, *kept) for chunk, kept in zip(CHUNKS, saved)]
     totals = chain("quad_total", quad, received[1], chain("quad_total", quad, received[0]))
     quads = lax.all_to_all(totals, "zq", split_axis=0, concat_axis=0, tiled=True)
     whole = chain("group_total", lax.axis_size("zq"), quads)

time: 214 us -> 217 us (1.014)
  waiting for transfers between devices: 72.5 us -> 69.1 us
  Pallas kernels: 57.4 us -> 59.8 us
    all_to_all x2, waiting for transfers between devices: 38.8 us -> 34.2 us  [local(): got = lax.all_to_all(maps, 'zi', split_axis=0, concat_axis=0, tiled=True)]
    pallas_call x5, Pallas kernels: 39.3 us -> 41.9 us  [the longest x2 21.5 us: block_maps(): pl.pallas_call(functools.partial(maps_kernel, first, heads, first), grid=...]
  transfers between devices with their start and end apart: 4 -> 4, of which waited for: 4 -> 3; matrix products, arithmetic and copies ran while one was open for 0% -> 0% of each run, Pallas kernels for 13% -> 15%
where the time goes in v3:
time: 217 us; the launch traced here: 214 us
  waiting for transfers between devices  69.1 us (32%)
  Pallas kernels  59.8 us (28%)
  blocking collectives  53 us (24%)
  starting transfers between devices  27.4 us (13%)
  local copies, waits for them, and re-layouts  3.7 us (2%)
    all_to_all x2, waiting for transfers between devices, local(): got = lax.all_to_all(maps, 'zi', split_axis=0, concat_axis=0, tiled=True)  34.2 us
    all_to_all x1, waiting for transfers between devices, local(): lax.all_to_all(totals, 'zq', split_axis=0, concat_axis=0, tiled=True)  28.8 us
    pallas_call x2, Pallas kernels, block_maps(): pl.pallas_call(functools.partial(maps_kernel, first, heads, first), grid=...  21.5 us
    all_to_all x1, blocking collectives, local(): mine = lax.all_to_all(starts, 'zq', split_axis=0, concat_axis=0, tiled=True)  19.8 us
    pallas_call x2, Pallas kernels, block_tokens(): pl.pallas_call(functools.partial(tokens_kernel, first), grid=(1,), in_spe...  15.7 us
    all_gather x1, blocking collectives, local(): lax.all_gather(chain('chip_total', lax.axis_size('core'), by_core)[0], 'y')  15.4 us
    all_gather x1, blocking collectives, local(): by_x = lax.all_gather(chain('y_total', lax.axis_size('y'), by_y)[0], 'x')  14.4 us
    all_to_all x1, starting transfers between devices, local(): lax.all_to_all(totals, 'zq', split_axis=0, concat_axis=0, tiled=True)  12.9 us
  transfers between devices with their start and end apart: 4, of which 3 were waited for; matrix products, arithmetic and copies ran while one was open for 0% of the time, Pallas kernels for 15%

profile of v3, /device:TPU:6, one launch (start us, length us, event | category | flops | bytes accessed | tf_op | source)
XLA Modules:
  0.0 213.8 jit_solution(10876388911120695525)
XLA Ops:
  0.0 6.5 %block_maps.2 = (f32[4,128,256]{2,1,0:T(8,128)}, f32[4,256,128]{2,1,0:T(8,128)}, f32[4,128,128]{2,1,0:T(8,128)}, f32[4,256]{1,0:T(4,128)}) custom-call(bf16[128,2,2048]{2,1,0:T(2,128)(2,1)} %k_ref.7, bf16[128,2,2048]{2,1,0:T(2,128)(2,1)} %v_ref.7, f32[2,16,128]{2,1,0:T(8,128)} %logit_ref.3), custom_call_target="tpu_custom_call" | custom-call | tf_op jit(solution)/shard_map/block_maps/pallas_call | solution.py:218
  6.5 5.9 %all-to-all-start.1 = ((f32[4,128,256]{2,1,0:T(8,128)}), f32[4,128,256]{2,1,0:T(8,128)S(1)}, u32[]{:S(2)}, u32[]{:S(2)}) async-start(f32[4,128,256]{2,1,0:T(8,128)} %get-tuple-element.28), calls=%async_computation.1 | async-start | bytes 1048576 | tf_op jit(solution)/shard_map/all_to_all | solution.py:437
  12.4 15.0 %block_maps.3 = (f32[12,128,256]{2,1,0:T(8,128)}, f32[12,256,128]{2,1,0:T(8,128)}, f32[12,128,128]{2,1,0:T(8,128)}, f32[12,256]{1,0:T(8,128)}) custom-call(bf16[128,2,2048]{2,1,0:T(2,128)(2,1)} %k_ref.7, bf16[128,2,2048]{2,1,0:T(2,128)(2,1)} %v_ref.7, f32[2,16,128]{2,1,0:T(8,128)} %logit_ref.3), custom_call_target="tpu_custom_call" | custom-call | tf_op jit(solution)/shard_map/block_maps/pallas_call | solution.py:218
  27.4 0.0 all-to-all-done.1.maps_ref.first_ref
  27.4 0.0 copy-start.2
  27.4 0.8 copy-done.2
  28.2 5.1 %all-to-all-start = ((f32[12,128,256]{2,1,0:T(8,128)}), f32[12,128,256]{2,1,0:T(8,128)S(1)}, u32[]{:S(2)}, u32[]{:S(2)}) async-start(f32[12,128,256]{2,1,0:T(8,128)} %get-tuple-element.27), calls=%async_computation | async-start | bytes 3145728 | tf_op jit(solution)/shard_map/all_to_all | solution.py:437
  33.3 2.2 %quad_total.2.refs_0_ = f32[1,128,256]{2,1,0:T(8,128)} custom-call(f32[4,128,256]{2,1,0:T(8,128)} %copy-done.2), custom_call_target="tpu_custom_call" | custom-call | tf_op jit(solution)/shard_map/quad_total/pallas_call | solution.py:324
  35.5 34.2 %all-to-all-done.maps_ref.second_ref = f32[12,128,256]{2,1,0:T(8,128)S(1)} async-done(((f32[12,128,256]{2,1,0:T(8,128)}), f32[12,128,256]{2,1,0:T(8,128)S(1)}, u32[]{:S(2)}, u32[]{:S(2)}) %all-to-all-start) | async-done | bytes 1572896 | tf_op jit(solution)/shard_map/all_to_all | solution.py:437
  69.7 0.0 copy-start
  69.7 1.1 copy-done
  70.8 2.9 %quad_total.3 = f32[4,128,256]{2,1,0:T(8,128)} custom-call(f32[12,128,256]{2,1,0:T(8,128)} %copy-done, f32[1,128,256]{2,1,0:T(8,128)} %quad_total.2.refs_0_), custom_call_target="tpu_custom_call" | custom-call | tf_op jit(solution)/shard_map/quad_total/pallas_call | solution.py:324
  73.7 12.9 %all-to-all-start.2 = ((f32[4,128,256]{2,1,0:T(8,128)}), f32[4,128,256]{2,1,0:T(8,128)S(1)}, u32[]{:S(2)}, u32[]{:S(2)}) async-start(f32[4,128,256]{2,1,0:T(8,128)} %quad_total.3), calls=%async_computation.2 | async-start | bytes 1048576 | tf_op jit(solution)/shard_map/all_to_all | solution.py:441
  86.7 0.6 pad_add_fusion.place_ref
  87.3 28.8 %all-to-all-done.2.maps_ref.quads_ref = f32[4,128,256]{2,1,0:T(8,128)S(1)} async-done(((f32[4,128,256]{2,1,0:T(8,128)}), f32[4,128,256]{2,1,0:T(8,128)S(1)}, u32[]{:S(2)}, u32[]{:S(2)}) %all-to-all-start.2) | async-done | bytes 524320 | tf_op jit(solution)/shard_map/all_to_all | solution.py:441
  116.0 0.0 copy-start.1
  116.0 0.8 copy-done.1
  116.8 2.2 %group_total.1 = f32[1,128,256]{2,1,0:T(8,128)} custom-call(f32[4,128,256]{2,1,0:T(8,128)} %copy-done.1), custom_call_target="tpu_custom_call" | custom-call | tf_op jit(solution)/shard_map/group_total/pallas_call | solution.py:324
  119.1 3.5 %all_gather.9.maps_ref.by_core_ref = f32[2,128,256]{2,1,0:T(8,128)} all-gather(f32[1,128,256]{2,1,0:T(8,128)} %group_total.1), channel_id=1, replica_groups=mesh['x'=4,'y'=4,'core'=2,'zq'=4,'zi'=4] {'core'}, dimensions={0}, use_global_device_ids=true | all-gather | bytes 393216 | tf_op jit(solution)/shard_map/all_gather | solution.py:443
  122.6 1.8 chip_total.1
  124.3 15.4 %all_gather.10.maps_ref.by_y_ref = f32[4,128,256]{2,1,0:T(8,128)} all-gather(f32[1,128,256]{2,1,0:T(8,128)} %chip_total.1), channel_id=1, replica_groups=mesh['x'=4,'y'=4,'core'=2,'zq'=4,'zi'=4] {'y'}, dimensions={0}, use_global_device_ids=true | all-gather | bytes 655360 | tf_op jit(solution)/shard_map/all_gather | solution.py:444
  139.7 2.3 %y_total.1 = f32[1,128,256]{2,1,0:T(8,128)} custom-call(f32[4,128,256]{2,1,0:T(8,128)} %all_gather.10.maps_ref.by_y_ref), custom_call_target="tpu_custom_call" | custom-call | tf_op jit(solution)/shard_map/y_total/pallas_call | solution.py:324
  142.0 14.4 %all_gather.11.by_x_ref = f32[4,128,256]{2,1,0:T(8,128)} all-gather(f32[1,128,256]{2,1,0:T(8,128)} %y_total.1), channel_id=1, replica_groups=mesh['x'=4,'y'=4,'core'=2,'zq'=4,'zi'=4] {'x'}, dimensions={0}, use_global_device_ids=true | all-gather | bytes 655360 | tf_op jit(solution)/shard_map/all_gather | solution.py:445
  156.4 3.2 %start_states.1 = f32[4,128,128]{2,1,0:T(8,128)} custom-call(s32[3]{0:T(128)} %pad_add_fusion.place_ref, f32[4,128,256]{2,1,0:T(8,128)} %all_gather.11.by_x_ref, f32[4,128,256]{2,1,0:T(8,128)} %all_gather.10.maps_ref.by_y_ref, f32[2,128,256]{2,1,0:T(8,128)} %all_gather.9.maps_ref.by_core_ref, f32[4,128,256]{2,1,0:T(8,128)} %copy-done.1), custom_call_target="tpu_custom_call" | custom-call | tf_op jit(solution)/shard_map/start_states/pallas_call | solution.py:347
  159.6 19.8 %all_to_all.25.start_ref = f32[4,128,128]{2,1,0:T(8,128)} all-to-all(f32[4,128,128]{2,1,0:T(8,128)} %start_states.1), channel_id=1, replica_groups=mesh['x'=4,'y'=4,'core'=2,'zq'=4,'zi'=4] {'zq'}, dimensions={0} | all-to-all | bytes 524288 | tf_op jit(solution)/shard_map/all_to_all | solution.py:448
  179.4 3.3 %spread.1 = f32[16,128,128]{2,1,0:T(8,128)} custom-call(f32[4,128,128]{2,1,0:T(8,128)} %all_to_all.25.start_ref, f32[4,128,256]{2,1,0:T(8,128)} %copy-done.2, f32[12,128,256]{2,1,0:T(8,128)} %copy-done), custom_call_target="tpu_custom_call" | custom-call | tf_op jit(solution)/shard_map/spread/pallas_call | solution.py:374
  182.7 3.5 %all-to-all-start.4 = ((f32[16,128,128]{2,1,0:T(8,128)}), f32[16,128,128]{2,1,0:T(8,128)S(1)}, u32[]{:S(2)}, u32[]{:S(2)}) async-start(f32[16,128,128]{2,1,0:T(8,128)} %spread.1), calls=%async_computation.4 | async-start | bytes 2097152 | tf_op jit(solution)/shard_map/all_to_all | solution.py:450
  186.2 4.7 %block_tokens.2 = (f32[4,128,128]{2,1,0:T(8,128)}, f32[4,128,128]{2,1,0:T(8,128)}) custom-call(bf16[128,2048]{1,0:T(8,128)(2,1)} %q_ref.3, bf16[128,2,2048]{2,1,0:T(2,128)(2,1)} %k_ref.7, bf16[128,2,2048]{2,1,0:T(2,128)(2,1)} %v_ref.7, f32[4,256,128]{2,1,0:T(8,128)} %get-tuple-element.17.inv_ref, f32[4,128,128]{2,1,0:T(8,128)} %get-tuple-element.18.cross_ref, ...), custom_call_target="tpu_custom_call" | custom-call | tf_op jit(solution)/shard_map/block_tokens/pallas_call | solution.py:271
  190.9 11.0 %block_tokens.3 = (f32[12,128,128]{2,1,0:T(8,128)}, f32[12,128,128]{2,1,0:T(8,128)}) custom-call(bf16[128,2048]{1,0:T(8,128)(2,1)} %q_ref.3, bf16[128,2,2048]{2,1,0:T(2,128)(2,1)} %k_ref.7, bf16[128,2,2048]{2,1,0:T(2,128)(2,1)} %v_ref.7, f32[12,256,128]{2,1,0:T(8,128)} %get-tuple-element.22.inv_ref, f32[12,128,128]{2,1,0:T(8,128)} %get-tuple-element.23.cross_ref, ...), custom_call_target="tpu_custom_call" | custom-call | tf_op jit(solution)/shard_map/block_tokens/pallas_call | solution.py:271
  201.9 6.2 %all-to-all-done.4.state_ref = f32[16,128,128]{2,1,0:T(8,128)S(1)} async-done(((f32[16,128,128]{2,1,0:T(8,128)}), f32[16,128,128]{2,1,0:T(8,128)S(1)}, u32[]{:S(2)}, u32[]{:S(2)}) %all-to-all-start.4) | async-done | bytes 1048608 | tf_op jit(solution)/shard_map/all_to_all | solution.py:450
  208.1 0.0 copy-start.3
  208.1 1.0 copy-done.3
  209.1 4.7 %finish.1 = bf16[128,2048]{1,0:T(8,128)(2,1)} custom-call(f32[4,128,128]{2,1,0:T(8,128)} %get-tuple-element.20.l0, f32[4,128,128]{2,1,0:T(8,128)} %get-tuple-element.21.c0, f32[12,128,128]{2,1,0:T(8,128)} %get-tuple-element.25.l1, f32[12,128,128]{2,1,0:T(8,128)} %get-tuple-element.26.c1, f32[16,128,128]{2,1,0:T(8,128)} %copy-done.3, f32[1,2048]{1,0:T(1,128)} %bitcast.4), custom_call_target="tpu_custom_call" | custom-call | tf_op jit(solution)/shard_map/finish/pallas_call | solution.py:419
Async XLA Ops:
  6.5 20.9 %all-to-all-start.1 = ((f32[4,128,256]{2,1,0:T(8,128)}), f32[4,128,256]{2,1,0:T(8,128)S(1)}, u32[]{:S(2)}, u32[]{:S(2)}) async-start(f32[4,128,256]{2,1,0:T(8,128)} %get-tuple-element.28), calls=%async_computation.1 | async-start | bytes 1048576 | tf_op jit(solution)/shard_map/all_to_all | solution.py:437
  27.4 0.8 copy-start.2
  28.2 41.5 %all-to-all-start = ((f32[12,128,256]{2,1,0:T(8,128)}), f32[12,128,256]{2,1,0:T(8,128)S(1)}, u32[]{:S(2)}, u32[]{:S(2)}) async-start(f32[12,128,256]{2,1,0:T(8,128)} %get-tuple-element.27), calls=%async_computation | async-start | bytes 3145728 | tf_op jit(solution)/shard_map/all_to_all | solution.py:437
  69.7 1.1 copy-start
  73.7 42.3 %all-to-all-start.2 = ((f32[4,128,256]{2,1,0:T(8,128)}), f32[4,128,256]{2,1,0:T(8,128)S(1)}, u32[]{:S(2)}, u32[]{:S(2)}) async-start(f32[4,128,256]{2,1,0:T(8,128)} %quad_total.3), calls=%async_computation.2 | async-start | bytes 1048576 | tf_op jit(solution)/shard_map/all_to_all | solution.py:441
  116.0 0.8 copy-start.1
  182.7 25.4 %all-to-all-start.4 = ((f32[16,128,128]{2,1,0:T(8,128)}), f32[16,128,128]{2,1,0:T(8,128)S(1)}, u32[]{:S(2)}, u32[]{:S(2)}) async-start(f32[16,128,128]{2,1,0:T(8,128)} %spread.1), calls=%async_computation.4 | async-start | bytes 2097152 | tf_op jit(solution)/shard_map/all_to_all | solution.py:450
  208.1 1.0 copy-start.3

commit v4 on v2

--- a/solution.py
+++ b/solution.py
@@ -12,7 +12,8 @@
 BASE = 16
 GROUP = 128 // BASE
 EPS = 1e-06
-VMEM = 56 * 1024 * 1024
+VMEM = 58 * 1024 * 1024
+SMALL = 16 * 1024 * 1024
 
 
 def parts(x):
@@ -47,6 +48,10 @@
 
 
 IN_VMEM = pl.BlockSpec(memory_space=pltpu.VMEM)
+
+
+def held_in_vmem(*arrays):
+    return [pltpu.with_memory_space_constraint(array, pltpu.VMEM) for array in arrays]
 
 
 def iota(shape, dim):
@@ -318,9 +323,9 @@
         in_specs=[IN_VMEM] * (1 + len(earlier)),
         out_specs=IN_VMEM,
         out_shape=jax.ShapeDtypeStruct((count,) + maps.shape[1:], F32),
-        compiler_params=pltpu.CompilerParams(vmem_limit_bytes=VMEM),
+        compiler_params=pltpu.CompilerParams(vmem_limit_bytes=SMALL),
         name=name,
-    )(maps, *earlier)
+    )(*held_in_vmem(maps, *earlier))
 
 
 def start_kernel(place_ref, by_x_ref, by_y_ref, by_core_ref, quads_ref, entry_ref):
@@ -341,9 +346,9 @@
         in_specs=[pl.BlockSpec(memory_space=pltpu.SMEM)] + [IN_VMEM] * 4,
         out_specs=IN_VMEM,
         out_shape=jax.ShapeDtypeStruct((count, size, size), F32),
-        compiler_params=pltpu.CompilerParams(vmem_limit_bytes=VMEM),
+        compiler_params=pltpu.CompilerParams(vmem_limit_bytes=SMALL),
         name="start_states",
-    )(place, by_x, by_y, by_core, quads)
+    )(place, *held_in_vmem(by_x, by_y, by_core, quads))
 
 
 def spread_kernel(start_ref, first_ref, second_ref, entry_ref):
@@ -366,9 +371,9 @@
         in_specs=[IN_VMEM] * 3,
         out_specs=IN_VMEM,
         out_shape=jax.ShapeDtypeStruct((members * heads, size, size), F32),
-        compiler_params=pltpu.CompilerParams(vmem_limit_bytes=VMEM),
+        compiler_params=pltpu.CompilerParams(vmem_limit_bytes=SMALL),
         name="spread",
-    )(start, first, second)
+    )(*held_in_vmem(start, first, second))
 
 
 def finish_kernel(lout_ref, cq_ref, states, gain_ref, out_ref):
@@ -421,7 +426,7 @@
         out_shape=jax.ShapeDtypeStruct((count, heads * size), BF16),
         compiler_params=pltpu.CompilerParams(vmem_limit_bytes=VMEM),
         name="finish",
-    )(lout0, cq0, lout1, cq1, state, gain.reshape(1, heads * size))
+    )(lout0, cq0, lout1, cq1, *held_in_vmem(state), gain.reshape(1, heads * size))
 
 
 def local(queries, keys, values, beta_logit, gain):

time: 214 us -> 195 us (0.911)
  Pallas kernels: 57.4 us -> 45.5 us
  blocking collectives: 52.1 us -> 46.7 us
  local copies, waits for them, and re-layouts: 3.74 us -> 0 us
  waiting for transfers between devices: 72.5 us -> 75.8 us
    pallas_call x5, Pallas kernels: 11.6 us -> 3.4 us  [chain(): pl.pallas_call(functools.partial(chain_kernel, pieces), in_specs=[IN_VMEM...]
    unnamed x8 -> x0, local copies, waits for them, and re-layouts: 3.74 us -> none
where the time goes in v4:
time: 195 us; the launch traced here: 194 us
  waiting for transfers between devices  75.8 us (39%)
  blocking collectives  46.7 us (24%)
  Pallas kernels  45.5 us (23%)
  starting transfers between devices  26.1 us (13%)
    all_to_all x2, waiting for transfers between devices, local(): got = lax.all_to_all(maps, 'zi', split_axis=0, concat_axis=0, tiled=True)  40.8 us
    all_to_all x1, waiting for transfers between devices, local(): lax.all_to_all(totals, 'zq', split_axis=0, concat_axis=0, tiled=True)  29.1 us
    pallas_call x2, Pallas kernels, block_maps(): pl.pallas_call(maps_kernel, grid=(1,), in_specs=[pl.BlockSpec((rows // 2,...  19 us
    all_to_all x1, blocking collectives, local(): mine = lax.all_to_all(starts, 'zq', split_axis=0, concat_axis=0, tiled=True)  18.6 us
    pallas_call x2, Pallas kernels, block_tokens(): pl.pallas_call(tokens_kernel, grid=(1,), in_specs=[pl.BlockSpec((count, l...  15.6 us
    all_gather x1, blocking collectives, local(): lax.all_gather(chain('chip_total', lax.axis_size('core'), by_core)[0], 'y')  13.3 us
    all_to_all x1, starting transfers between devices, local(): lax.all_to_all(totals, 'zq', split_axis=0, concat_axis=0, tiled=True)  13 us
    all_gather x1, blocking collectives, local(): by_x = lax.all_gather(chain('y_total', lax.axis_size('y'), by_y)[0], 'x')  12.8 us
  transfers between devices with their start and end apart: 4, of which 4 were waited for; matrix products, arithmetic and copies ran while one was open for 0% of the time, Pallas kernels for 13%

profile of v4, /device:TPU:6, one launch (start us, length us, event | category | flops | bytes accessed | tf_op | source)
XLA Modules:
  0.0 194.2 jit_solution(10830591721604377866)
XLA Ops:
  0.0 9.5 %block_maps.2 = (f32[8,128,256]{2,1,0:T(8,128)}, f32[8,256,128]{2,1,0:T(8,128)}, f32[8,128,128]{2,1,0:T(8,128)}, f32[8,256]{1,0:T(8,128)}) custom-call(bf16[128,2,2048]{2,1,0:T(2,128)(2,1)} %k_ref.7, bf16[128,2,2048]{2,1,0:T(2,128)(2,1)} %v_ref.7, f32[2,16,128]{2,1,0:T(8,128)} %logit_ref.3), custom_call_target="tpu_custom_call" | custom-call | tf_op jit(solution)/shard_map/block_maps/pallas_call | solution.py:215
  9.5 5.9 %all-to-all-start.1 = ((f32[8,128,256]{2,1,0:T(8,128)}), f32[8,128,256]{2,1,0:T(8,128)S(1)}, u32[]{:S(2)}, u32[]{:S(2)}) async-start(f32[8,128,256]{2,1,0:T(8,128)} %get-tuple-element.28), calls=%async_computation.1 | async-start | bytes 2097152 | tf_op jit(solution)/shard_map/all_to_all | solution.py:439
  15.4 9.5 %block_maps.3 = (f32[8,128,256]{2,1,0:T(8,128)}, f32[8,256,128]{2,1,0:T(8,128)}, f32[8,128,128]{2,1,0:T(8,128)}, f32[8,256]{1,0:T(8,128)}) custom-call(bf16[128,2,2048]{2,1,0:T(2,128)(2,1)} %k_ref.7, bf16[128,2,2048]{2,1,0:T(2,128)(2,1)} %v_ref.7, f32[2,16,128]{2,1,0:T(8,128)} %logit_ref.3), custom_call_target="tpu_custom_call" | custom-call | tf_op jit(solution)/shard_map/block_maps/pallas_call | solution.py:215
  24.9 16.2 %all-to-all-done.1.maps_ref.first_ref = f32[8,128,256]{2,1,0:T(8,128)S(1)} async-done(((f32[8,128,256]{2,1,0:T(8,128)}), f32[8,128,256]{2,1,0:T(8,128)S(1)}, u32[]{:S(2)}, u32[]{:S(2)}) %all-to-all-start.1) | async-done | bytes 1048608 | tf_op jit(solution)/shard_map/all_to_all | solution.py:439
  41.1 3.5 %all-to-all-start = ((f32[8,128,256]{2,1,0:T(8,128)}), f32[8,128,256]{2,1,0:T(8,128)S(1)}, u32[]{:S(2)}, u32[]{:S(2)}) async-start(f32[8,128,256]{2,1,0:T(8,128)} %get-tuple-element.27), calls=%async_computation | async-start | bytes 2097152 | tf_op jit(solution)/shard_map/all_to_all | solution.py:439
  44.6 0.6 quad_total.2.refs_0_
  45.3 24.5 %all-to-all-done.maps_ref.second_ref = f32[8,128,256]{2,1,0:T(8,128)S(1)} async-done(((f32[8,128,256]{2,1,0:T(8,128)}), f32[8,128,256]{2,1,0:T(8,128)S(1)}, u32[]{:S(2)}, u32[]{:S(2)}) %all-to-all-start) | async-done | bytes 1048608 | tf_op jit(solution)/shard_map/all_to_all | solution.py:439
  69.8 1.4 quad_total.3
  71.3 13.0 %all-to-all-start.2 = ((f32[4,128,256]{2,1,0:T(8,128)}), f32[4,128,256]{2,1,0:T(8,128)S(1)}, u32[]{:S(2)}, u32[]{:S(2)}) async-start(f32[4,128,256]{2,1,0:T(8,128)} %quad_total.3), calls=%async_computation.2 | async-start | bytes 1048576 | tf_op jit(solution)/shard_map/all_to_all | solution.py:443
  84.3 0.1 pad_add_fusion.place_ref
  84.3 29.1 %all-to-all-done.2.maps_ref.quads_ref = f32[4,128,256]{2,1,0:T(8,128)S(1)} async-done(((f32[4,128,256]{2,1,0:T(8,128)}), f32[4,128,256]{2,1,0:T(8,128)S(1)}, u32[]{:S(2)}, u32[]{:S(2)}) %all-to-all-start.2) | async-done | bytes 524320 | tf_op jit(solution)/shard_map/all_to_all | solution.py:443
  113.5 0.6 group_total.1
  114.1 2.0 %all_gather.9.maps_ref.by_core_ref = f32[2,128,256]{2,1,0:T(8,128)S(1)} all-gather(f32[1,128,256]{2,1,0:T(8,128)S(1)} %group_total.1), channel_id=1, replica_groups=mesh['x'=4,'y'=4,'core'=2,'zq'=4,'zi'=4] {'core'}, dimensions={0}, use_global_device_ids=true | all-gather | bytes 393216 | tf_op jit(solution)/shard_map/all_gather | solution.py:445
  116.1 0.2 chip_total.1
  116.2 13.3 %all_gather.10.maps_ref.by_y_ref = f32[4,128,256]{2,1,0:T(8,128)S(1)} all-gather(f32[1,128,256]{2,1,0:T(8,128)S(1)} %chip_total.1), channel_id=1, replica_groups=mesh['x'=4,'y'=4,'core'=2,'zq'=4,'zi'=4] {'y'}, dimensions={0}, use_global_device_ids=true | all-gather | bytes 655360 | tf_op jit(solution)/shard_map/all_gather | solution.py:446
  129.5 0.6 y_total.1
  130.1 12.8 %all_gather.11.by_x_ref = f32[4,128,256]{2,1,0:T(8,128)S(1)} all-gather(f32[1,128,256]{2,1,0:T(8,128)S(1)} %y_total.1), channel_id=1, replica_groups=mesh['x'=4,'y'=4,'core'=2,'zq'=4,'zi'=4] {'x'}, dimensions={0}, use_global_device_ids=true | all-gather | bytes 655360 | tf_op jit(solution)/shard_map/all_gather | solution.py:447
  142.9 1.6 start_states.1
  144.5 18.6 %all_to_all.25.start_ref = f32[4,128,128]{2,1,0:T(8,128)S(1)} all-to-all(f32[4,128,128]{2,1,0:T(8,128)S(1)} %start_states.1), channel_id=1, replica_groups=mesh['x'=4,'y'=4,'core'=2,'zq'=4,'zi'=4] {'zq'}, dimensions={0} | all-to-all | bytes 524288 | tf_op jit(solution)/shard_map/all_to_all | solution.py:450
  163.1 1.6 spread.1
  164.7 3.7 %all-to-all-start.4 = ((f32[16,128,128]{2,1,0:T(8,128)}), f32[16,128,128]{2,1,0:T(8,128)S(1)}, u32[]{:S(2)}, u32[]{:S(2)}) async-start(f32[16,128,128]{2,1,0:T(8,128)} %spread.1), calls=%async_computation.4 | async-start | bytes 2097152 | tf_op jit(solution)/shard_map/all_to_all | solution.py:452
  168.5 7.8 %block_tokens.3 = (f32[8,128,128]{2,1,0:T(8,128)}, f32[8,128,128]{2,1,0:T(8,128)}) custom-call(bf16[128,2048]{1,0:T(8,128)(2,1)} %q_ref.3, bf16[128,2,2048]{2,1,0:T(2,128)(2,1)} %k_ref.7, bf16[128,2,2048]{2,1,0:T(2,128)(2,1)} %v_ref.7, f32[8,256,128]{2,1,0:T(8,128)} %get-tuple-element.22.inv_ref, f32[8,128,128]{2,1,0:T(8,128)} %get-tuple-element.23.cross_ref, ...), custom_call_target="tpu_custom_call" | custom-call | tf_op jit(solution)/shard_map/block_tokens/pallas_call | solution.py:268
  176.2 7.8 %block_tokens.2 = (f32[8,128,128]{2,1,0:T(8,128)}, f32[8,128,128]{2,1,0:T(8,128)}) custom-call(bf16[128,2048]{1,0:T(8,128)(2,1)} %q_ref.3, bf16[128,2,2048]{2,1,0:T(2,128)(2,1)} %k_ref.7, bf16[128,2,2048]{2,1,0:T(2,128)(2,1)} %v_ref.7, f32[8,256,128]{2,1,0:T(8,128)} %get-tuple-element.17.inv_ref, f32[8,128,128]{2,1,0:T(8,128)} %get-tuple-element.18.cross_ref, ...), custom_call_target="tpu_custom_call" | custom-call | tf_op jit(solution)/shard_map/block_tokens/pallas_call | solution.py:268
  184.0 5.9 %all-to-all-done.4.state_ref = f32[16,128,128]{2,1,0:T(8,128)S(1)} async-done(((f32[16,128,128]{2,1,0:T(8,128)}), f32[16,128,128]{2,1,0:T(8,128)S(1)}, u32[]{:S(2)}, u32[]{:S(2)}) %all-to-all-start.4) | async-done | bytes 1048608 | tf_op jit(solution)/shard_map/all_to_all | solution.py:452
  189.9 4.3 %finish.1 = bf16[128,2048]{1,0:T(8,128)(2,1)} custom-call(f32[8,128,128]{2,1,0:T(8,128)} %get-tuple-element.20.l0, f32[8,128,128]{2,1,0:T(8,128)} %get-tuple-element.21.c0, f32[8,128,128]{2,1,0:T(8,128)} %get-tuple-element.25.l1, f32[8,128,128]{2,1,0:T(8,128)} %get-tuple-element.26.c1, f32[16,128,128]{2,1,0:T(8,128)S(1)} %all-to-all-done.4.state_ref, ...), custom_call_target="tpu_custom_call" | custom-call | tf_op jit(solution)/shard_map/finish/pallas_call | solution.py:414
Async XLA Ops:
  9.5 31.6 %all-to-all-start.1 = ((f32[8,128,256]{2,1,0:T(8,128)}), f32[8,128,256]{2,1,0:T(8,128)S(1)}, u32[]{:S(2)}, u32[]{:S(2)}) async-start(f32[8,128,256]{2,1,0:T(8,128)} %get-tuple-element.28), calls=%async_computation.1 | async-start | bytes 2097152 | tf_op jit(solution)/shard_map/all_to_all | solution.py:439
  41.1 28.7 %all-to-all-start = ((f32[8,128,256]{2,1,0:T(8,128)}), f32[8,128,256]{2,1,0:T(8,128)S(1)}, u32[]{:S(2)}, u32[]{:S(2)}) async-start(f32[8,128,256]{2,1,0:T(8,128)} %get-tuple-element.27), calls=%async_computation | async-start | bytes 2097152 | tf_op jit(solution)/shard_map/all_to_all | solution.py:439
  71.3 42.2 %all-to-all-start.2 = ((f32[4,128,256]{2,1,0:T(8,128)}), f32[4,128,256]{2,1,0:T(8,128)S(1)}, u32[]{:S(2)}, u32[]{:S(2)}) async-start(f32[4,128,256]{2,1,0:T(8,128)} %quad_total.3), calls=%async_computation.2 | async-start | bytes 1048576 | tf_op jit(solution)/shard_map/all_to_all | solution.py:443
  164.7 25.2 %all-to-all-start.4 = ((f32[16,128,128]{2,1,0:T(8,128)}), f32[16,128,128]{2,1,0:T(8,128)S(1)}, u32[]{:S(2)}, u32[]{:S(2)}) async-start(f32[16,128,128]{2,1,0:T(8,128)} %spread.1), calls=%async_computation.4 | async-start | bytes 2097152 | tf_op jit(solution)/shard_map/all_to_all | solution.py:452

commit v5 on v4

--- a/solution.py
+++ b/solution.py
@@ -328,6 +328,84 @@
     )(*held_in_vmem(maps, *earlier))
 
 
+def send_kernel(place_ref, maps_ref, earlier_ref, own_ref, right_ref, left_ref):
+    size = maps_ref.shape[1]
+    early = earlier_ref.shape[0]
+    per = early
+    pieces = maps_ref.shape[0] // per
+    accs = [maps_ref[j] for j in range(per)]
+    for i in range(1, pieces):
+        accs = [after(maps_ref[i * per + j], acc) for j, acc in enumerate(accs)]
+    totals = [earlier_ref[j] for j in range(early)] + accs
+    me = place_ref[3]
+
+    def pick(ahead):
+        at = lax.rem(me + ahead, len(totals))
+        found = totals[0]
+        for j in range(1, len(totals)):
+            found = jnp.where(at == j, totals[j], found)
+        return found
+
+    own_ref[...] = pick(0)
+    ahead, opposite, behind = pick(1), pick(2), pick(3)
+    right_ref[0] = ahead[:, :size]
+    right_ref[1] = ahead[:, size:]
+    right_ref[2] = opposite[:, :size]
+    left_ref[0] = behind[:, :size]
+    left_ref[1] = behind[:, size:]
+    left_ref[2] = opposite[:, size:]
+
+
+def quad_sends(place, maps, earlier):
+    size, wide = maps.shape[1:]
+    return pl.pallas_call(
+        send_kernel,
+        in_specs=[pl.BlockSpec(memory_space=pltpu.SMEM)] + [IN_VMEM] * 2,
+        out_specs=[IN_VMEM] * 3,
+        out_shape=[
+            jax.ShapeDtypeStruct((size, wide), F32),
+            jax.ShapeDtypeStruct((3, size, size), F32),
+            jax.ShapeDtypeStruct((3, size, size), F32),
+        ],
+        compiler_params=pltpu.CompilerParams(vmem_limit_bytes=SMALL),
+        name="quad_sends",
+    )(place, *held_in_vmem(maps, earlier))
+
+
+def gather_kernel(place_ref, own_ref, near_left_ref, near_right_ref, far_a_ref, far_b_ref, quads_ref, total_ref):
+    size = own_ref.shape[0]
+    count = quads_ref.shape[0]
+    me = place_ref[3]
+    quads_ref[me] = own_ref[...]
+    for ahead, first, second in (
+        (1, near_right_ref[0], near_right_ref[1]),
+        (2, far_a_ref[...], far_b_ref[...]),
+        (3, near_left_ref[0], near_left_ref[1]),
+    ):
+        at = lax.rem(me + ahead, count)
+        quads_ref[at, :, :size] = first
+        quads_ref[at, :, size:] = second
+    acc = quads_ref[0]
+    for i in range(1, count):
+        acc = after(quads_ref[i], acc)
+    total_ref[...] = acc
+
+
+def gather_quads(place, own, near_left, near_right, far_a, far_b):
+    size, wide = own.shape
+    return pl.pallas_call(
+        gather_kernel,
+        in_specs=[pl.BlockSpec(memory_space=pltpu.SMEM)] + [IN_VMEM] * 5,
+        out_specs=[IN_VMEM] * 2,
+        out_shape=[
+            jax.ShapeDtypeStruct((4, size, wide), F32),
+            jax.ShapeDtypeStruct((size, wide), F32),
+        ],
+        compiler_params=pltpu.CompilerParams(vmem_limit_bytes=SMALL),
+        name="gather_quads",
+    )(place, *held_in_vmem(own, near_left, near_right, far_a, far_b))
+
+
 def start_kernel(place_ref, by_x_ref, by_y_ref, by_core_ref, quads_ref, entry_ref):
     size = by_x_ref.shape[1]
     state = jnp.zeros((size, size), F32)
@@ -439,13 +517,19 @@
         got = lax.all_to_all(maps, "zi", split_axis=0, concat_axis=0, tiled=True)
         received.append(got)
     tokens = [block_tokens(group, queries, keys, values, *saved[group]) for group in range(2)]
-    totals = chain("quad_total", quad, received[1], chain("quad_total", quad, received[0]))
-    quads = lax.all_to_all(totals, "zq", split_axis=0, concat_axis=0, tiled=True)
-    whole = chain("group_total", lax.axis_size("zq"), quads)
-    by_core = lax.all_gather(whole[0], "core")
+    place = jnp.stack([lax.axis_index(axis) for axis in ("x", "y", "core", "zq")])
+    ring = lax.axis_size("zq")
+    rightward = [(i, (i + 1) % ring) for i in range(ring)]
+    leftward = [(i, (i - 1) % ring) for i in range(ring)]
+    own, to_right, to_left = quad_sends(place, received[1], chain("quad_total", quad, received[0]))
+    from_left = lax.ppermute(to_right, "zq", rightward)
+    from_right = lax.ppermute(to_left, "zq", leftward)
+    far_a = lax.ppermute(from_left[2], "zq", rightward)
+    far_b = lax.ppermute(from_right[2], "zq", leftward)
+    quads, whole = gather_quads(place, own, from_left, from_right, far_a, far_b)
+    by_core = lax.all_gather(whole, "core")
     by_y = lax.all_gather(chain("chip_total", lax.axis_size("core"), by_core)[0], "y")
     by_x = lax.all_gather(chain("y_total", lax.axis_size("y"), by_y)[0], "x")
-    place = jnp.stack([lax.axis_index("x"), lax.axis_index("y"), lax.axis_index("core")])
     starts = start_states(place, by_x, by_y, by_core, quads)
     mine = lax.all_to_all(starts, "zq", split_axis=0, concat_axis=0, tiled=True)
     entries = spread(mine, received[0], received[1])

time: 195 us -> 202 us (1.036)
  starting transfers between devices: 26.1 us -> 35.4 us
  waiting for transfers between devices: 75.8 us -> 67.7 us
  blocking collectives: 46.7 us -> 52.5 us
    all_to_all x1 -> x0, waiting for transfers between devices: 29.1 us -> none  [local(): lax.all_to_all(totals, 'zq', split_axis=0, concat_axis=0, tiled=True)]
    ppermute x0 -> x4, starting transfers between devices: none -> 22.3 us  [the longest x1 9.09 us: local(): from_left = lax.ppermute(to_right, 'zq', rightward)]
    ppermute x0 -> x4, waiting for transfers between devices: none -> 19 us  [the longest x1 15.1 us: local(): from_left = lax.ppermute(to_right, 'zq', rightward)]
    all_to_all x1 -> x0, starting transfers between devices: 13 us -> none  [local(): lax.all_to_all(totals, 'zq', split_axis=0, concat_axis=0, tiled=True)]
    all_to_all x1, blocking collectives: 18.6 us -> 24.4 us  [local(): mine = lax.all_to_all(starts, 'zq', split_axis=0, concat_axis=0, tiled=True)]
    pallas_call x0 -> x2, Pallas kernels: none -> 2.37 us  [the longest x1 1.21 us: quad_sends(): pl.pallas_call(send_kernel, in_specs=[pl.BlockSpec(memory_space=pltpu.SME...]
    all_to_all x1, waiting for transfers between devices: 5.88 us -> 7.98 us  [local(): lax.all_to_all(entries, 'zi', split_axis=0, concat_axis=0, tiled=True)]
  transfers between devices with their start and end apart: 4 -> 7, of which waited for: 4 -> 6; matrix products, arithmetic and copies ran while one was open for 0% -> 0% of each run, Pallas kernels for 13% -> 13%
where the time goes in v5:
time: 202 us
  waiting for transfers between devices  67.7 us (34%)
  blocking collectives  52.5 us (26%)
  Pallas kernels  45.8 us (23%)
  starting transfers between devices  35.4 us (18%)
    all_to_all x2, waiting for transfers between devices, local(): got = lax.all_to_all(maps, 'zi', split_axis=0, concat_axis=0, tiled=True)  40.7 us
    all_to_all x1, blocking collectives, local(): mine = lax.all_to_all(starts, 'zq', split_axis=0, concat_axis=0, tiled=True)  24.4 us
    pallas_call x2, Pallas kernels, block_maps(): pl.pallas_call(maps_kernel, grid=(1,), in_specs=[pl.BlockSpec((rows // 2,...  19 us
    pallas_call x2, Pallas kernels, block_tokens(): pl.pallas_call(tokens_kernel, grid=(1,), in_specs=[pl.BlockSpec((count, l...  15.6 us
    ppermute x1, waiting for transfers between devices, local(): from_left = lax.ppermute(to_right, 'zq', rightward)  15.1 us
    all_gather x1, blocking collectives, local(): lax.all_gather(chain('chip_total', lax.axis_size('core'), by_core)[0], 'y')  13.3 us
    all_gather x1, blocking collectives, local(): by_x = lax.all_gather(chain('y_total', lax.axis_size('y'), by_y)[0], 'x')  12.8 us
    all_to_all x2, starting transfers between devices, local(): got = lax.all_to_all(maps, 'zi', split_axis=0, concat_axis=0, tiled=True)  9.41 us
  transfers between devices with their start and end apart: 7, of which 6 were waited for; matrix products, arithmetic and copies ran while one was open for 0% of the time, Pallas kernels for 13%

profile of v5, /device:TPU:6, one launch (start us, length us, event | category | flops | bytes accessed | tf_op | source)
XLA Modules:
  0.0 201.7 jit_solution(486095540966189892)
XLA Ops:
  0.0 9.5 %block_maps.2 = (f32[8,128,256]{2,1,0:T(8,128)}, f32[8,256,128]{2,1,0:T(8,128)}, f32[8,128,128]{2,1,0:T(8,128)}, f32[8,256]{1,0:T(8,128)}) custom-call(bf16[128,2,2048]{2,1,0:T(2,128)(2,1)} %k_ref.7, bf16[128,2,2048]{2,1,0:T(2,128)(2,1)} %v_ref.7, f32[2,16,128]{2,1,0:T(8,128)} %logit_ref.3), custom_call_target="tpu_custom_call" | custom-call | tf_op jit(solution)/shard_map/block_maps/pallas_call | solution.py:215
  9.5 5.9 %all-to-all-start.1 = ((f32[8,128,256]{2,1,0:T(8,128)}), f32[8,128,256]{2,1,0:T(8,128)S(1)}, u32[]{:S(2)}, u32[]{:S(2)}) async-start(f32[8,128,256]{2,1,0:T(8,128)} %get-tuple-element.33), calls=%async_computation.1 | async-start | bytes 2097152 | tf_op jit(solution)/shard_map/all_to_all | solution.py:517
  15.4 9.5 %block_maps.3 = (f32[8,128,256]{2,1,0:T(8,128)}, f32[8,256,128]{2,1,0:T(8,128)}, f32[8,128,128]{2,1,0:T(8,128)}, f32[8,256]{1,0:T(8,128)}) custom-call(bf16[128,2,2048]{2,1,0:T(2,128)(2,1)} %k_ref.7, bf16[128,2,2048]{2,1,0:T(2,128)(2,1)} %v_ref.7, f32[2,16,128]{2,1,0:T(8,128)} %logit_ref.3), custom_call_target="tpu_custom_call" | custom-call | tf_op jit(solution)/shard_map/block_maps/pallas_call | solution.py:215
  24.9 16.2 %all-to-all-done.1.maps_ref.first_ref = f32[8,128,256]{2,1,0:T(8,128)S(1)} async-done(((f32[8,128,256]{2,1,0:T(8,128)}), f32[8,128,256]{2,1,0:T(8,128)S(1)}, u32[]{:S(2)}, u32[]{:S(2)}) %all-to-all-start.1) | async-done | bytes 1048608 | tf_op jit(solution)/shard_map/all_to_all | solution.py:517
  41.1 3.5 %all-to-all-start = ((f32[8,128,256]{2,1,0:T(8,128)}), f32[8,128,256]{2,1,0:T(8,128)S(1)}, u32[]{:S(2)}, u32[]{:S(2)}) async-start(f32[8,128,256]{2,1,0:T(8,128)} %get-tuple-element.32), calls=%async_computation | async-start | bytes 2097152 | tf_op jit(solution)/shard_map/all_to_all | solution.py:517
  44.7 0.1 pad_add_fusion.place_ref
  44.7 0.6 quad_total.1.earlier_ref
  45.4 24.5 %all-to-all-done.maps_ref.second_ref = f32[8,128,256]{2,1,0:T(8,128)S(1)} async-done(((f32[8,128,256]{2,1,0:T(8,128)}), f32[8,128,256]{2,1,0:T(8,128)S(1)}, u32[]{:S(2)}, u32[]{:S(2)}) %all-to-all-start) | async-done | bytes 1048608 | tf_op jit(solution)/shard_map/all_to_all | solution.py:517
  69.9 1.2 quad_sends.1
  71.1 9.1 %collective-permute-start = (f32[3,128,128]{2,1,0:T(8,128)S(1)}, f32[3,128,128]{2,1,0:T(8,128)S(1)}, u32[]{:S(2)}, u32[]{:S(2)}) collective-permute-start(f32[3,128,128]{2,1,0:T(8,128)S(1)} %get-tuple-element.35), channel_id=1, source_target_pairs={{0,4},{4,8},{8,12},{12,0},{1,5},{5,9},{9,13},{13,1},{2,6},{6,10},{... | collective-permute-start | bytes 589832 | tf_op jit(solution)/shard_map/ppermute | solution.py:525
  80.2 3.5 %collective-permute-start.1 = (f32[3,128,128]{2,1,0:T(8,128)S(1)}, f32[3,128,128]{2,1,0:T(8,128)S(1)}, u32[]{:S(2)}, u32[]{:S(2)}) collective-permute-start(f32[3,128,128]{2,1,0:T(8,128)S(1)} %get-tuple-element.36), channel_id=1, source_target_pairs={{0,12},{4,0},{8,4},{12,8},{1,13},{5,1},{9,5},{13,9},{2,14},{6,2},{... | collective-permute-start | bytes 589832 | tf_op jit(solution)/shard_map/ppermute | solution.py:526
  83.6 15.1 %collective-permute-done.near_left_ref = f32[3,128,128]{2,1,0:T(8,128)S(1)} collective-permute-done((f32[3,128,128]{2,1,0:T(8,128)S(1)}, f32[3,128,128]{2,1,0:T(8,128)S(1)}, u32[]{:S(2)}, u32[]{:S(2)}) %collective-permute-start) | collective-permute-done | bytes 196640 | tf_op jit(solution)/shard_map/ppermute | solution.py:525
  98.7 3.6 %collective-permute-start.2 = (f32[128,128]{1,0:T(8,128)S(1)}, f32[128,128]{1,0:T(8,128)S(1)}, u32[]{:S(2)}, u32[]{:S(2)}) collective-permute-start(f32[128,128]{1,0:T(8,128)S(1)} %slice_bitcast_fusion.1), channel_id=1, source_target_pairs={{0,4},{4,8},{8,12},{12,0},{1,5},{5,9},{9,13},{13,1},{2,6},{6,10},{... | collective-permute-start | bytes 196616 | tf_op jit(solution)/shard_map/ppermute | solution.py:527
  102.4 0.0 collective-permute-done.1.near_right_ref
  102.4 6.1 %collective-permute-start.3 = (f32[128,128]{1,0:T(8,128)S(1)}, f32[128,128]{1,0:T(8,128)S(1)}, u32[]{:S(2)}, u32[]{:S(2)}) collective-permute-start(f32[128,128]{1,0:T(8,128)S(1)} %slice_bitcast_fusion), channel_id=1, source_target_pairs={{0,12},{4,0},{8,4},{12,8},{1,13},{5,1},{9,5},{13,9},{2,14},{6,2},{... | collective-permute-start | bytes 196616 | tf_op jit(solution)/shard_map/ppermute | solution.py:528
  108.5 0.4 collective-permute-done.2.far_a_ref
  108.9 3.6 %collective-permute-done.3.far_b_ref = f32[128,128]{1,0:T(8,128)S(1)} collective-permute-done((f32[128,128]{1,0:T(8,128)S(1)}, f32[128,128]{1,0:T(8,128)S(1)}, u32[]{:S(2)}, u32[]{:S(2)}) %collective-permute-start.3) | collective-permute-done | bytes 65568 | tf_op jit(solution)/shard_map/ppermute | solution.py:528
  112.5 1.2 gather_quads.1
  113.6 2.0 all-gather
  115.6 0.2 chip_total.1
  115.8 13.3 %all_gather.14.maps_ref.by_y_ref = f32[4,128,256]{2,1,0:T(8,128)S(1)} all-gather(f32[1,128,256]{2,1,0:T(8,128)S(1)} %chip_total.1), channel_id=1, replica_groups=mesh['x'=4,'y'=4,'core'=2,'zq'=4,'zi'=4] {'y'}, dimensions={0}, use_global_device_ids=true | all-gather | bytes 655360 | tf_op jit(solution)/shard_map/all_gather | solution.py:531
  129.1 0.6 y_total.1
  129.7 12.8 %all_gather.15.by_x_ref = f32[4,128,256]{2,1,0:T(8,128)S(1)} all-gather(f32[1,128,256]{2,1,0:T(8,128)S(1)} %y_total.1), channel_id=1, replica_groups=mesh['x'=4,'y'=4,'core'=2,'zq'=4,'zi'=4] {'x'}, dimensions={0}, use_global_device_ids=true | all-gather | bytes 655360 | tf_op jit(solution)/shard_map/all_gather | solution.py:532
  142.5 1.6 start_states.1
  144.1 24.4 %all_to_all.20.start_ref = f32[4,128,128]{2,1,0:T(8,128)S(1)} all-to-all(f32[4,128,128]{2,1,0:T(8,128)S(1)} %start_states.1), channel_id=1, replica_groups=mesh['x'=4,'y'=4,'core'=2,'zq'=4,'zi'=4] {'zq'}, dimensions={0} | all-to-all | bytes 524288 | tf_op jit(solution)/shard_map/all_to_all | solution.py:534
  168.5 1.6 spread.1
  170.1 3.7 %all-to-all-start.3 = ((f32[16,128,128]{2,1,0:T(8,128)}), f32[16,128,128]{2,1,0:T(8,128)S(1)}, u32[]{:S(2)}, u32[]{:S(2)}) async-start(f32[16,128,128]{2,1,0:T(8,128)} %spread.1), calls=%async_computation.3 | async-start | bytes 2097152 | tf_op jit(solution)/shard_map/all_to_all | solution.py:536
  173.9 7.8 %block_tokens.3 = (f32[8,128,128]{2,1,0:T(8,128)}, f32[8,128,128]{2,1,0:T(8,128)}) custom-call(bf16[128,2048]{1,0:T(8,128)(2,1)} %q_ref.3, bf16[128,2,2048]{2,1,0:T(2,128)(2,1)} %k_ref.7, bf16[128,2,2048]{2,1,0:T(2,128)(2,1)} %v_ref.7, f32[8,256,128]{2,1,0:T(8,128)} %get-tuple-element.27.inv_ref, f32[8,128,128]{2,1,0:T(8,128)} %get-tuple-element.28.cross_ref, ...), custom_call_target="tpu_custom_call" | custom-call | tf_op jit(solution)/shard_map/block_tokens/pallas_call | solution.py:268
  181.7 7.8 %block_tokens.2 = (f32[8,128,128]{2,1,0:T(8,128)}, f32[8,128,128]{2,1,0:T(8,128)}) custom-call(bf16[128,2048]{1,0:T(8,128)(2,1)} %q_ref.3, bf16[128,2,2048]{2,1,0:T(2,128)(2,1)} %k_ref.7, bf16[128,2,2048]{2,1,0:T(2,128)(2,1)} %v_ref.7, f32[8,256,128]{2,1,0:T(8,128)} %get-tuple-element.22.inv_ref, f32[8,128,128]{2,1,0:T(8,128)} %get-tuple-element.23.cross_ref, ...), custom_call_target="tpu_custom_call" | custom-call | tf_op jit(solution)/shard_map/block_tokens/pallas_call | solution.py:268
  189.4 8.0 %all-to-all-done.3.state_ref = f32[16,128,128]{2,1,0:T(8,128)S(1)} async-done(((f32[16,128,128]{2,1,0:T(8,128)}), f32[16,128,128]{2,1,0:T(8,128)S(1)}, u32[]{:S(2)}, u32[]{:S(2)}) %all-to-all-start.3) | async-done | bytes 1048608 | tf_op jit(solution)/shard_map/all_to_all | solution.py:536
  197.4 4.3 %finish.1 = bf16[128,2048]{1,0:T(8,128)(2,1)} custom-call(f32[8,128,128]{2,1,0:T(8,128)} %get-tuple-element.25.l0, f32[8,128,128]{2,1,0:T(8,128)} %get-tuple-element.26.c0, f32[8,128,128]{2,1,0:T(8,128)} %get-tuple-element.30.l1, f32[8,128,128]{2,1,0:T(8,128)} %get-tuple-element.31.c1, f32[16,128,128]{2,1,0:T(8,128)S(1)} %all-to-all-done.3.state_ref, ...), custom_call_target="tpu_custom_call" | custom-call | tf_op jit(solution)/shard_map/finish/pallas_call | solution.py:492
  (2 shorter events, 0.0 us)
Async XLA Ops:
  9.5 31.6 %all-to-all-start.1 = ((f32[8,128,256]{2,1,0:T(8,128)}), f32[8,128,256]{2,1,0:T(8,128)S(1)}, u32[]{:S(2)}, u32[]{:S(2)}) async-start(f32[8,128,256]{2,1,0:T(8,128)} %get-tuple-element.33), calls=%async_computation.1 | async-start | bytes 2097152 | tf_op jit(solution)/shard_map/all_to_all | solution.py:517
  41.1 28.7 %all-to-all-start = ((f32[8,128,256]{2,1,0:T(8,128)}), f32[8,128,256]{2,1,0:T(8,128)S(1)}, u32[]{:S(2)}, u32[]{:S(2)}) async-start(f32[8,128,256]{2,1,0:T(8,128)} %get-tuple-element.32), calls=%async_computation | async-start | bytes 2097152 | tf_op jit(solution)/shard_map/all_to_all | solution.py:517
  71.1 27.7 %collective-permute-start = (f32[3,128,128]{2,1,0:T(8,128)S(1)}, f32[3,128,128]{2,1,0:T(8,128)S(1)}, u32[]{:S(2)}, u32[]{:S(2)}) collective-permute-start(f32[3,128,128]{2,1,0:T(8,128)S(1)} %get-tuple-element.35), channel_id=1, source_target_pairs={{0,4},{4,8},{8,12},{12,0},{1,5},{5,9},{9,13},{13,1},{2,6},{6,10},{... | collective-permute-start | bytes 589832 | tf_op jit(solution)/shard_map/ppermute | solution.py:525
  80.2 22.2 %collective-permute-start.1 = (f32[3,128,128]{2,1,0:T(8,128)S(1)}, f32[3,128,128]{2,1,0:T(8,128)S(1)}, u32[]{:S(2)}, u32[]{:S(2)}) collective-permute-start(f32[3,128,128]{2,1,0:T(8,128)S(1)} %get-tuple-element.36), channel_id=1, source_target_pairs={{0,12},{4,0},{8,4},{12,8},{1,13},{5,1},{9,5},{13,9},{2,14},{6,2},{... | collective-permute-start | bytes 589832 | tf_op jit(solution)/shard_map/ppermute | solution.py:526
  98.7 10.1 %collective-permute-start.2 = (f32[128,128]{1,0:T(8,128)S(1)}, f32[128,128]{1,0:T(8,128)S(1)}, u32[]{:S(2)}, u32[]{:S(2)}) collective-permute-start(f32[128,128]{1,0:T(8,128)S(1)} %slice_bitcast_fusion.1), channel_id=1, source_target_pairs={{0,4},{4,8},{8,12},{12,0},{1,5},{5,9},{9,13},{13,1},{2,6},{6,10},{... | collective-permute-start | bytes 196616 | tf_op jit(solution)/shard_map/ppermute | solution.py:527
  102.4 10.1 %collective-permute-start.3 = (f32[128,128]{1,0:T(8,128)S(1)}, f32[128,128]{1,0:T(8,128)S(1)}, u32[]{:S(2)}, u32[]{:S(2)}) collective-permute-start(f32[128,128]{1,0:T(8,128)S(1)} %slice_bitcast_fusion), channel_id=1, source_target_pairs={{0,12},{4,0},{8,4},{12,8},{1,13},{5,1},{9,5},{13,9},{2,14},{6,2},{... | collective-permute-start | bytes 196616 | tf_op jit(solution)/shard_map/ppermute | solution.py:528
  170.1 27.3 %all-to-all-start.3 = ((f32[16,128,128]{2,1,0:T(8,128)}), f32[16,128,128]{2,1,0:T(8,128)S(1)}, u32[]{:S(2)}, u32[]{:S(2)}) async-start(f32[16,128,128]{2,1,0:T(8,128)} %spread.1), calls=%async_computation.3 | async-start | bytes 2097152 | tf_op jit(solution)/shard_map/all_to_all | solution.py:536

commit v6 on v4

--- a/solution.py
+++ b/solution.py
@@ -302,6 +302,27 @@
     return times_map(piece, state) + piece[:, piece.shape[0] :]
 
 
+def placed_chain_kernel(pieces, place_ref, maps_ref, total_ref, placed_ref):
+    for axis in range(place_ref.shape[0]):
+        placed_ref[axis] = place_ref[axis]
+    chain_kernel(pieces, maps_ref, total_ref)
+
+
+def placed_chain(name, pieces, maps, place):
+    smem = pl.BlockSpec(memory_space=pltpu.SMEM)
+    return pl.pallas_call(
+        functools.partial(placed_chain_kernel, pieces),
+        in_specs=[smem, IN_VMEM],
+        out_specs=[IN_VMEM, smem],
+        out_shape=[
+            jax.ShapeDtypeStruct((maps.shape[0] // pieces,) + maps.shape[1:], F32),
+            jax.ShapeDtypeStruct(place.shape, place.dtype),
+        ],
+        compiler_params=pltpu.CompilerParams(vmem_limit_bytes=SMALL),
+        name=name,
+    )(place, *held_in_vmem(maps))
+
+
 def chain_kernel(pieces, maps_ref, *refs):
     total_ref = refs[-1]
     heads = maps_ref.shape[0] // pieces
@@ -439,13 +460,14 @@
         got = lax.all_to_all(maps, "zi", split_axis=0, concat_axis=0, tiled=True)
         received.append(got)
     tokens = [block_tokens(group, queries, keys, values, *saved[group]) for group in range(2)]
-    totals = chain("quad_total", quad, received[1], chain("quad_total", quad, received[0]))
+    place = jnp.stack([lax.axis_index("x"), lax.axis_index("y"), lax.axis_index("core")])
+    early, place = placed_chain("quad_total", quad, received[0], place)
+    totals = chain("quad_total", quad, received[1], early)
     quads = lax.all_to_all(totals, "zq", split_axis=0, concat_axis=0, tiled=True)
     whole = chain("group_total", lax.axis_size("zq"), quads)
     by_core = lax.all_gather(whole[0], "core")
     by_y = lax.all_gather(chain("chip_total", lax.axis_size("core"), by_core)[0], "y")
     by_x = lax.all_gather(chain("y_total", lax.axis_size("y"), by_y)[0], "x")
-    place = jnp.stack([lax.axis_index("x"), lax.axis_index("y"), lax.axis_index("core")])
     starts = start_states(place, by_x, by_y, by_core, quads)
     mine = lax.all_to_all(starts, "zq", split_axis=0, concat_axis=0, tiled=True)
     entries = spread(mine, received[0], received[1])

time: 195 us -> 196 us (level)
  blocking collectives: 46.7 us -> 89.8 us
  waiting for transfers between devices: 75.8 us -> 47.6 us
  starting transfers between devices: 26.1 us -> 13.1 us
    all_to_all x0 -> x1, blocking collectives: none -> 42 us  [local(): lax.all_to_all(totals, 'zq', split_axis=0, concat_axis=0, tiled=True)]
    all_to_all x1 -> x0, waiting for transfers between devices: 29.1 us -> none  [local(): lax.all_to_all(totals, 'zq', split_axis=0, concat_axis=0, tiled=True)]
    all_to_all x1 -> x0, starting transfers between devices: 13 us -> none  [local(): lax.all_to_all(totals, 'zq', split_axis=0, concat_axis=0, tiled=True)]
  transfers between devices with their start and end apart: 4 -> 3, of which waited for: 4 -> 3; matrix products, arithmetic and copies ran while one was open for 0% -> 0% of each run, Pallas kernels for 13% -> 13%
where the time goes in v6:
time: 196 us
  blocking collectives  89.8 us (46%)
  waiting for transfers between devices  47.6 us (24%)
  Pallas kernels  45.2 us (23%)
  starting transfers between devices  13.1 us (7%)
    all_to_all x1, blocking collectives, local(): lax.all_to_all(totals, 'zq', split_axis=0, concat_axis=0, tiled=True)  42 us
    all_to_all x2, waiting for transfers between devices, local(): got = lax.all_to_all(maps, 'zi', split_axis=0, concat_axis=0, tiled=True)  40.1 us
    all_to_all x1, blocking collectives, local(): mine = lax.all_to_all(starts, 'zq', split_axis=0, concat_axis=0, tiled=True)  19.7 us
    pallas_call x2, Pallas kernels, block_maps(): pl.pallas_call(maps_kernel, grid=(1,), in_specs=[pl.BlockSpec((rows // 2,...  19 us
    pallas_call x2, Pallas kernels, block_tokens(): pl.pallas_call(tokens_kernel, grid=(1,), in_specs=[pl.BlockSpec((count, l...  15.6 us
    all_gather x1, blocking collectives, local(): lax.all_gather(chain('chip_total', lax.axis_size('core'), by_core)[0], 'y')  13.3 us
    all_gather x1, blocking collectives, local(): by_x = lax.all_gather(chain('y_total', lax.axis_size('y'), by_y)[0], 'x')  12.8 us
    all_to_all x2, starting transfers between devices, local(): got = lax.all_to_all(maps, 'zi', split_axis=0, concat_axis=0, tiled=True)  9.41 us
  transfers between devices with their start and end apart: 3, of which 3 were waited for; matrix products, arithmetic and copies ran while one was open for 0% of the time, Pallas kernels for 13%

profile of v6, /device:TPU:6, one launch (start us, length us, event | category | flops | bytes accessed | tf_op | source)
XLA Modules:
  0.0 195.9 jit_solution(5172224441309193909)
XLA Ops:
  0.0 9.5 %block_maps.2 = (f32[8,128,256]{2,1,0:T(8,128)}, f32[8,256,128]{2,1,0:T(8,128)}, f32[8,128,128]{2,1,0:T(8,128)}, f32[8,256]{1,0:T(8,128)}) custom-call(bf16[128,2,2048]{2,1,0:T(2,128)(2,1)} %k_ref.7, bf16[128,2,2048]{2,1,0:T(2,128)(2,1)} %v_ref.7, f32[2,16,128]{2,1,0:T(8,128)} %logit_ref.3), custom_call_target="tpu_custom_call" | custom-call | tf_op jit(solution)/shard_map/block_maps/pallas_call | solution.py:215
  9.5 5.9 %all-to-all-start = ((f32[8,128,256]{2,1,0:T(8,128)}), f32[8,128,256]{2,1,0:T(8,128)S(1)}, u32[]{:S(2)}, u32[]{:S(2)}) async-start(f32[8,128,256]{2,1,0:T(8,128)} %get-tuple-element.29), calls=%async_computation | async-start | bytes 2097152 | tf_op jit(solution)/shard_map/all_to_all | solution.py:460
  15.4 9.5 %block_maps.3 = (f32[8,128,256]{2,1,0:T(8,128)}, f32[8,256,128]{2,1,0:T(8,128)}, f32[8,128,128]{2,1,0:T(8,128)}, f32[8,256]{1,0:T(8,128)}) custom-call(bf16[128,2,2048]{2,1,0:T(2,128)(2,1)} %k_ref.7, bf16[128,2,2048]{2,1,0:T(2,128)(2,1)} %v_ref.7, f32[2,16,128]{2,1,0:T(8,128)} %logit_ref.3), custom_call_target="tpu_custom_call" | custom-call | tf_op jit(solution)/shard_map/block_maps/pallas_call | solution.py:215
  24.9 16.2 %all-to-all-done.maps_ref.first_ref = f32[8,128,256]{2,1,0:T(8,128)S(1)} async-done(((f32[8,128,256]{2,1,0:T(8,128)}), f32[8,128,256]{2,1,0:T(8,128)S(1)}, u32[]{:S(2)}, u32[]{:S(2)}) %all-to-all-start) | async-done | bytes 1048608 | tf_op jit(solution)/shard_map/all_to_all | solution.py:460
  41.1 3.5 %all-to-all-start.1 = ((f32[8,128,256]{2,1,0:T(8,128)}), f32[8,128,256]{2,1,0:T(8,128)S(1)}, u32[]{:S(2)}, u32[]{:S(2)}) async-start(f32[8,128,256]{2,1,0:T(8,128)} %get-tuple-element.31), calls=%async_computation.1 | async-start | bytes 2097152 | tf_op jit(solution)/shard_map/all_to_all | solution.py:460
  44.7 0.1 pad_add_fusion.place_ref
  44.7 1.2 quad_total.2
  45.9 23.9 %all-to-all-done.1.maps_ref.second_ref = f32[8,128,256]{2,1,0:T(8,128)S(1)} async-done(((f32[8,128,256]{2,1,0:T(8,128)}), f32[8,128,256]{2,1,0:T(8,128)S(1)}, u32[]{:S(2)}, u32[]{:S(2)}) %all-to-all-start.1) | async-done | bytes 1048608 | tf_op jit(solution)/shard_map/all_to_all | solution.py:460
  69.8 0.7 quad_total.3
  70.5 42.0 %all_to_all.25.maps_ref.quads_ref = f32[4,128,256]{2,1,0:T(8,128)S(1)} all-to-all(f32[4,128,256]{2,1,0:T(8,128)S(1)} %quad_total.3), channel_id=1, replica_groups=mesh['x'=4,'y'=4,'core'=2,'zq'=4,'zi'=4] {'zq'}, dimensions={0} | all-to-all | bytes 1048576 | tf_op jit(solution)/shard_map/all_to_all | solution.py:466
  112.5 0.6 group_total.1
  113.1 2.0 %all_gather.9.maps_ref.by_core_ref = f32[2,128,256]{2,1,0:T(8,128)S(1)} all-gather(f32[1,128,256]{2,1,0:T(8,128)S(1)} %group_total.1), channel_id=1, replica_groups=mesh['x'=4,'y'=4,'core'=2,'zq'=4,'zi'=4] {'core'}, dimensions={0}, use_global_device_ids=true | all-gather | bytes 393216 | tf_op jit(solution)/shard_map/all_gather | solution.py:468
  115.1 0.2 chip_total.1
  115.3 13.3 %all_gather.10.maps_ref.by_y_ref = f32[4,128,256]{2,1,0:T(8,128)S(1)} all-gather(f32[1,128,256]{2,1,0:T(8,128)S(1)} %chip_total.1), channel_id=1, replica_groups=mesh['x'=4,'y'=4,'core'=2,'zq'=4,'zi'=4] {'y'}, dimensions={0}, use_global_device_ids=true | all-gather | bytes 655360 | tf_op jit(solution)/shard_map/all_gather | solution.py:469
  128.6 0.6 y_total.1
  129.1 12.8 %all_gather.11.by_x_ref = f32[4,128,256]{2,1,0:T(8,128)S(1)} all-gather(f32[1,128,256]{2,1,0:T(8,128)S(1)} %y_total.1), channel_id=1, replica_groups=mesh['x'=4,'y'=4,'core'=2,'zq'=4,'zi'=4] {'x'}, dimensions={0}, use_global_device_ids=true | all-gather | bytes 655360 | tf_op jit(solution)/shard_map/all_gather | solution.py:470
  141.9 1.6 start_states.1
  143.5 19.7 %all_to_all.26.start_ref = f32[4,128,128]{2,1,0:T(8,128)S(1)} all-to-all(f32[4,128,128]{2,1,0:T(8,128)S(1)} %start_states.1), channel_id=1, replica_groups=mesh['x'=4,'y'=4,'core'=2,'zq'=4,'zi'=4] {'zq'}, dimensions={0} | all-to-all | bytes 524288 | tf_op jit(solution)/shard_map/all_to_all | solution.py:472
  163.2 1.6 spread.1
  164.8 3.7 %all-to-all-start.4 = ((f32[16,128,128]{2,1,0:T(8,128)}), f32[16,128,128]{2,1,0:T(8,128)S(1)}, u32[]{:S(2)}, u32[]{:S(2)}) async-start(f32[16,128,128]{2,1,0:T(8,128)} %spread.1), calls=%async_computation.4 | async-start | bytes 2097152 | tf_op jit(solution)/shard_map/all_to_all | solution.py:474
  168.6 7.8 %block_tokens.3 = (f32[8,128,128]{2,1,0:T(8,128)}, f32[8,128,128]{2,1,0:T(8,128)}) custom-call(bf16[128,2048]{1,0:T(8,128)(2,1)} %q_ref.3, bf16[128,2,2048]{2,1,0:T(2,128)(2,1)} %k_ref.7, bf16[128,2,2048]{2,1,0:T(2,128)(2,1)} %v_ref.7, f32[8,256,128]{2,1,0:T(8,128)} %get-tuple-element.24.inv_ref, f32[8,128,128]{2,1,0:T(8,128)} %get-tuple-element.25.cross_ref, ...), custom_call_target="tpu_custom_call" | custom-call | tf_op jit(solution)/shard_map/block_tokens/pallas_call | solution.py:268
  176.3 7.8 %block_tokens.2 = (f32[8,128,128]{2,1,0:T(8,128)}, f32[8,128,128]{2,1,0:T(8,128)}) custom-call(bf16[128,2048]{1,0:T(8,128)(2,1)} %q_ref.3, bf16[128,2,2048]{2,1,0:T(2,128)(2,1)} %k_ref.7, bf16[128,2,2048]{2,1,0:T(2,128)(2,1)} %v_ref.7, f32[8,256,128]{2,1,0:T(8,128)} %get-tuple-element.19.inv_ref, f32[8,128,128]{2,1,0:T(8,128)} %get-tuple-element.20.cross_ref, ...), custom_call_target="tpu_custom_call" | custom-call | tf_op jit(solution)/shard_map/block_tokens/pallas_call | solution.py:268
  184.1 7.5 %all-to-all-done.4.state_ref = f32[16,128,128]{2,1,0:T(8,128)S(1)} async-done(((f32[16,128,128]{2,1,0:T(8,128)}), f32[16,128,128]{2,1,0:T(8,128)S(1)}, u32[]{:S(2)}, u32[]{:S(2)}) %all-to-all-start.4) | async-done | bytes 1048608 | tf_op jit(solution)/shard_map/all_to_all | solution.py:474
  191.6 4.3 %finish.1 = bf16[128,2048]{1,0:T(8,128)(2,1)} custom-call(f32[8,128,128]{2,1,0:T(8,128)} %get-tuple-element.22.l0, f32[8,128,128]{2,1,0:T(8,128)} %get-tuple-element.23.c0, f32[8,128,128]{2,1,0:T(8,128)} %get-tuple-element.27.l1, f32[8,128,128]{2,1,0:T(8,128)} %get-tuple-element.28.c1, f32[16,128,128]{2,1,0:T(8,128)S(1)} %all-to-all-done.4.state_ref, ...), custom_call_target="tpu_custom_call" | custom-call | tf_op jit(solution)/shard_map/finish/pallas_call | solution.py:435
Async XLA Ops:
  9.5 31.6 %all-to-all-start = ((f32[8,128,256]{2,1,0:T(8,128)}), f32[8,128,256]{2,1,0:T(8,128)S(1)}, u32[]{:S(2)}, u32[]{:S(2)}) async-start(f32[8,128,256]{2,1,0:T(8,128)} %get-tuple-element.29), calls=%async_computation | async-start | bytes 2097152 | tf_op jit(solution)/shard_map/all_to_all | solution.py:460
  41.1 28.7 %all-to-all-start.1 = ((f32[8,128,256]{2,1,0:T(8,128)}), f32[8,128,256]{2,1,0:T(8,128)S(1)}, u32[]{:S(2)}, u32[]{:S(2)}) async-start(f32[8,128,256]{2,1,0:T(8,128)} %get-tuple-element.31), calls=%async_computation.1 | async-start | bytes 2097152 | tf_op jit(solution)/shard_map/all_to_all | solution.py:460
  164.8 26.8 %all-to-all-start.4 = ((f32[16,128,128]{2,1,0:T(8,128)}), f32[16,128,128]{2,1,0:T(8,128)S(1)}, u32[]{:S(2)}, u32[]{:S(2)}) async-start(f32[16,128,128]{2,1,0:T(8,128)} %spread.1), calls=%async_computation.4 | async-start | bytes 2097152 | tf_op jit(solution)/shard_map/all_to_all | solution.py:474

commit v7 on v4

--- a/solution.py
+++ b/solution.py
@@ -328,18 +328,45 @@
     )(*held_in_vmem(maps, *earlier))
 
 
-def start_kernel(place_ref, by_x_ref, by_y_ref, by_core_ref, quads_ref, entry_ref):
-    size = by_x_ref.shape[1]
-    state = jnp.zeros((size, size), F32)
-    for axis, ref in enumerate((by_x_ref, by_y_ref, by_core_ref)):
-        state = lax.fori_loop(0, place_ref[axis], lambda i, s, ref=ref: advance(ref[i], s), state)
+def copies_kernel(core_ref, by_core_ref, copies_ref):
+    size = by_core_ref.shape[1]
+    chip = after(by_core_ref[1], by_core_ref[0])
+    half = jnp.where(core_ref[0] == 0, chip[:, :size], chip[:, size:])
+    for i in range(copies_ref.shape[0]):
+        copies_ref[i] = half
+
+
+def chip_copies(core, by_core, chips):
+    size = by_core.shape[1]
+    return pl.pallas_call(
+        copies_kernel,
+        in_specs=[pl.BlockSpec(memory_space=pltpu.SMEM), IN_VMEM],
+        out_specs=IN_VMEM,
+        out_shape=jax.ShapeDtypeStruct((chips, size, size), F32),
+        compiler_params=pltpu.CompilerParams(vmem_limit_bytes=SMALL),
+        name="chip_copies",
+    )(core, *held_in_vmem(by_core))
+
+
+def start_kernel(place_ref, mine_ref, other_ref, by_core_ref, quads_ref, entry_ref):
+    size = mine_ref.shape[1]
+    first = place_ref[1] == 0
+
+    def by_chip(i, state):
+        mine, other = mine_ref[i], other_ref[i]
+        transition = jnp.where(first, mine, other)
+        offset = jnp.where(first, other, mine)
+        return times_map(transition, state) + offset
+
+    state = lax.fori_loop(0, place_ref[0], by_chip, jnp.zeros((size, size), F32))
+    state = jnp.where(first, state, advance(by_core_ref[0], state))
     entry_ref[0] = state
     for i in range(quads_ref.shape[0] - 1):
         state = advance(quads_ref[i], state)
         entry_ref[i + 1] = state
 
 
-def start_states(place, by_x, by_y, by_core, quads):
+def start_states(place, mine, other, by_core, quads):
     count, size, _ = quads.shape
     return pl.pallas_call(
         start_kernel,
@@ -348,7 +375,7 @@
         out_shape=jax.ShapeDtypeStruct((count, size, size), F32),
         compiler_params=pltpu.CompilerParams(vmem_limit_bytes=SMALL),
         name="start_states",
-    )(place, *held_in_vmem(by_x, by_y, by_core, quads))
+    )(place, *held_in_vmem(mine, other, by_core, quads))
 
 
 def spread_kernel(start_ref, first_ref, second_ref, entry_ref):
@@ -443,12 +470,15 @@
     quads = lax.all_to_all(totals, "zq", split_axis=0, concat_axis=0, tiled=True)
     whole = chain("group_total", lax.axis_size("zq"), quads)
     by_core = lax.all_gather(whole[0], "core")
-    by_y = lax.all_gather(chain("chip_total", lax.axis_size("core"), by_core)[0], "y")
-    by_x = lax.all_gather(chain("y_total", lax.axis_size("y"), by_y)[0], "x")
-    place = jnp.stack([lax.axis_index("x"), lax.axis_index("y"), lax.axis_index("core")])
-    starts = start_states(place, by_x, by_y, by_core, quads)
-    mine = lax.all_to_all(starts, "zq", split_axis=0, concat_axis=0, tiled=True)
-    entries = spread(mine, received[0], received[1])
+    core = lax.axis_index("core")
+    chips = lax.axis_size("x") * lax.axis_size("y")
+    copies = chip_copies(core.reshape(1), by_core, chips)
+    mine = lax.all_to_all(copies, ("x", "y"), split_axis=0, concat_axis=0, tiled=True)
+    other = lax.ppermute(mine, "core", [(0, 1), (1, 0)])
+    place = jnp.stack([lax.axis_index(("x", "y")), core])
+    starts = start_states(place, mine, other, by_core, quads)
+    held = lax.all_to_all(starts, "zq", split_axis=0, concat_axis=0, tiled=True)
+    entries = spread(held, received[0], received[1])
     state = lax.all_to_all(entries, "zi", split_axis=0, concat_axis=0, tiled=True)
     return finish(tokens, state, gain)
 

time: 195 us -> 204 us (1.046)
  waiting for transfers between devices: 75.8 us -> 81.5 us
  starting transfers between devices: 26.1 us -> 29 us
  Pallas kernels: 45.5 us -> 47.7 us
    all_gather x2 -> x0, blocking collectives: 26.1 us -> none  [the longest x1 13.3 us: local(): lax.all_gather(chain('chip_total', lax.axis_size('core'), by_core)[0], 'y')]
    all_to_all x1 -> x2, blocking collectives: 18.6 us -> 43.2 us  [the longest x1 22.7 us: local(): lax.all_to_all(copies, ('x', 'y'), split_axis=0, concat_axis=0, tiled=True)]
    ppermute x0 -> x1, waiting for transfers between devices: none -> 2.88 us  [local(): other = lax.ppermute(mine, 'core', [(0, 1), (1, 0)])]
    all_to_all x1, waiting for transfers between devices: 5.88 us -> 8.64 us  [local(): lax.all_to_all(entries, 'zi', split_axis=0, concat_axis=0, tiled=True)]
    pallas_call x1, Pallas kernels: 1.59 us -> 4.31 us  [start_states(): pl.pallas_call(start_kernel, in_specs=[pl.BlockSpec(memory_space=pltpu.SM...]
  transfers between devices with their start and end apart: 4 -> 5, of which waited for: 4 -> 5; matrix products, arithmetic and copies ran while one was open for 0% -> 0% of each run, Pallas kernels for 13% -> 13%
where the time goes in v7:
time: 204 us
  waiting for transfers between devices  81.5 us (40%)
  Pallas kernels  47.7 us (23%)
  blocking collectives  45.2 us (22%)
  starting transfers between devices  29 us (14%)
    all_to_all x2, waiting for transfers between devices, local(): got = lax.all_to_all(maps, 'zi', split_axis=0, concat_axis=0, tiled=True)  40.8 us
    all_to_all x1, waiting for transfers between devices, local(): lax.all_to_all(totals, 'zq', split_axis=0, concat_axis=0, tiled=True)  29.2 us
    all_to_all x1, blocking collectives, local(): lax.all_to_all(copies, ('x', 'y'), split_axis=0, concat_axis=0, tiled=True)  22.7 us
    all_to_all x1, blocking collectives, local(): held = lax.all_to_all(starts, 'zq', split_axis=0, concat_axis=0, tiled=True)  20.5 us
    pallas_call x2, Pallas kernels, block_maps(): pl.pallas_call(maps_kernel, grid=(1,), in_specs=[pl.BlockSpec((rows // 2,...  19 us
    pallas_call x2, Pallas kernels, block_tokens(): pl.pallas_call(tokens_kernel, grid=(1,), in_specs=[pl.BlockSpec((count, l...  15.6 us
    all_to_all x1, starting transfers between devices, local(): lax.all_to_all(totals, 'zq', split_axis=0, concat_axis=0, tiled=True)  13 us
    all_to_all x2, starting transfers between devices, local(): got = lax.all_to_all(maps, 'zi', split_axis=0, concat_axis=0, tiled=True)  9.41 us
  transfers between devices with their start and end apart: 5, of which 5 were waited for; matrix products, arithmetic and copies ran while one was open for 0% of the time, Pallas kernels for 13%

profile of v7, /device:TPU:6, one launch (start us, length us, event | category | flops | bytes accessed | tf_op | source)
XLA Modules:
  0.0 203.6 jit_solution(5645379924650597542)
XLA Ops:
  0.0 9.5 %block_maps.2 = (f32[8,128,256]{2,1,0:T(8,128)}, f32[8,256,128]{2,1,0:T(8,128)}, f32[8,128,128]{2,1,0:T(8,128)}, f32[8,256]{1,0:T(8,128)}) custom-call(bf16[128,2,2048]{2,1,0:T(2,128)(2,1)} %k_ref.7, bf16[128,2,2048]{2,1,0:T(2,128)(2,1)} %v_ref.7, f32[2,16,128]{2,1,0:T(8,128)} %logit_ref.3), custom_call_target="tpu_custom_call" | custom-call | tf_op jit(solution)/shard_map/block_maps/pallas_call | solution.py:215
  9.5 5.9 %all-to-all-start.1 = ((f32[8,128,256]{2,1,0:T(8,128)}), f32[8,128,256]{2,1,0:T(8,128)S(1)}, u32[]{:S(2)}, u32[]{:S(2)}) async-start(f32[8,128,256]{2,1,0:T(8,128)} %get-tuple-element.28), calls=%async_computation.1 | async-start | bytes 2097152 | tf_op jit(solution)/shard_map/all_to_all | solution.py:466
  15.4 9.5 %block_maps.3 = (f32[8,128,256]{2,1,0:T(8,128)}, f32[8,256,128]{2,1,0:T(8,128)}, f32[8,128,128]{2,1,0:T(8,128)}, f32[8,256]{1,0:T(8,128)}) custom-call(bf16[128,2,2048]{2,1,0:T(2,128)(2,1)} %k_ref.7, bf16[128,2,2048]{2,1,0:T(2,128)(2,1)} %v_ref.7, f32[2,16,128]{2,1,0:T(8,128)} %logit_ref.3), custom_call_target="tpu_custom_call" | custom-call | tf_op jit(solution)/shard_map/block_maps/pallas_call | solution.py:215
  24.9 16.2 %all-to-all-done.1.maps_ref.first_ref = f32[8,128,256]{2,1,0:T(8,128)S(1)} async-done(((f32[8,128,256]{2,1,0:T(8,128)}), f32[8,128,256]{2,1,0:T(8,128)S(1)}, u32[]{:S(2)}, u32[]{:S(2)}) %all-to-all-start.1) | async-done | bytes 1048608 | tf_op jit(solution)/shard_map/all_to_all | solution.py:466
  41.1 3.5 %all-to-all-start = ((f32[8,128,256]{2,1,0:T(8,128)}), f32[8,128,256]{2,1,0:T(8,128)S(1)}, u32[]{:S(2)}, u32[]{:S(2)}) async-start(f32[8,128,256]{2,1,0:T(8,128)} %get-tuple-element.27), calls=%async_computation | async-start | bytes 2097152 | tf_op jit(solution)/shard_map/all_to_all | solution.py:466
  44.6 0.6 quad_total.2.refs_0_
  45.3 24.5 %all-to-all-done.maps_ref.second_ref = f32[8,128,256]{2,1,0:T(8,128)S(1)} async-done(((f32[8,128,256]{2,1,0:T(8,128)}), f32[8,128,256]{2,1,0:T(8,128)S(1)}, u32[]{:S(2)}, u32[]{:S(2)}) %all-to-all-start) | async-done | bytes 1048608 | tf_op jit(solution)/shard_map/all_to_all | solution.py:466
  69.8 1.5 quad_total.3
  71.3 13.0 %all-to-all-start.2 = ((f32[4,128,256]{2,1,0:T(8,128)}), f32[4,128,256]{2,1,0:T(8,128)S(1)}, u32[]{:S(2)}, u32[]{:S(2)}) async-start(f32[4,128,256]{2,1,0:T(8,128)} %quad_total.3), calls=%async_computation.2 | async-start | bytes 1048576 | tf_op jit(solution)/shard_map/all_to_all | solution.py:470
  84.3 29.2 %all-to-all-done.2.maps_ref.quads_ref = f32[4,128,256]{2,1,0:T(8,128)S(1)} async-done(((f32[4,128,256]{2,1,0:T(8,128)}), f32[4,128,256]{2,1,0:T(8,128)S(1)}, u32[]{:S(2)}, u32[]{:S(2)}) %all-to-all-start.2) | async-done | bytes 524320 | tf_op jit(solution)/shard_map/all_to_all | solution.py:470
  113.5 0.6 group_total.1
  114.1 2.0 all_gather.3.by_core_ref
  116.1 0.3 chip_copies.1
  116.3 22.7 %all_to_all.30.mine_ref = f32[16,128,128]{2,1,0:T(8,128)} all-to-all(f32[16,128,128]{2,1,0:T(8,128)S(1)} %chip_copies.1), channel_id=1, replica_groups=mesh['x'=4,'y'=4,'core'=2,'zq'=4,'zi'=4] {'x','y'}, dimensions={0} | all-to-all | bytes 2097152 | tf_op jit(solution)/shard_map/all_to_all | solution.py:476
  139.0 1.9 collective-permute-start
  140.9 0.1 pad_add_fusion.place_ref
  141.0 2.9 %collective-permute-done.other_ref = f32[16,128,128]{2,1,0:T(8,128)} collective-permute-done((f32[16,128,128]{2,1,0:T(8,128)}, f32[16,128,128]{2,1,0:T(8,128)}, u32[]{:S(2)}, u32[]{:S(2)}) %collective-permute-start) | collective-permute-done | bytes 1048608 | tf_op jit(solution)/shard_map/ppermute | solution.py:477
  143.9 4.3 %start_states.1 = f32[4,128,128]{2,1,0:T(8,128)S(1)} custom-call(s32[2]{0:T(128)S(1)} %pad_add_fusion.place_ref, f32[16,128,128]{2,1,0:T(8,128)} %all_to_all.30.mine_ref, f32[16,128,128]{2,1,0:T(8,128)} %collective-permute-done.other_ref, f32[2,128,256]{2,1,0:T(8,128)S(1)} %all_gather.3.by_core_ref, f32[4,128,256]{2,1,0:T(8,128)S(1)} %all-to-all-done.2.maps_ref.quads_ref), custom_call_target="tpu_custom_call" | custom-call | tf_op jit(solution)/shard_map/start_states/pallas_call | solution.py:371
  148.2 20.5 %all_to_all.31.start_ref = f32[4,128,128]{2,1,0:T(8,128)S(1)} all-to-all(f32[4,128,128]{2,1,0:T(8,128)S(1)} %start_states.1), channel_id=1, replica_groups=mesh['x'=4,'y'=4,'core'=2,'zq'=4,'zi'=4] {'zq'}, dimensions={0} | all-to-all | bytes 524288 | tf_op jit(solution)/shard_map/all_to_all | solution.py:480
  168.7 1.6 spread.1
  170.3 4.7 %all-to-all-start.5 = ((f32[16,128,128]{2,1,0:T(8,128)}), f32[16,128,128]{2,1,0:T(8,128)S(1)}, u32[]{:S(2)}, u32[]{:S(2)}) async-start(f32[16,128,128]{2,1,0:T(8,128)} %spread.1), calls=%async_computation.5 | async-start | bytes 2097152 | tf_op jit(solution)/shard_map/all_to_all | solution.py:482
  175.1 7.8 %block_tokens.3 = (f32[8,128,128]{2,1,0:T(8,128)}, f32[8,128,128]{2,1,0:T(8,128)}) custom-call(bf16[128,2048]{1,0:T(8,128)(2,1)} %q_ref.3, bf16[128,2,2048]{2,1,0:T(2,128)(2,1)} %k_ref.7, bf16[128,2,2048]{2,1,0:T(2,128)(2,1)} %v_ref.7, f32[8,256,128]{2,1,0:T(8,128)} %get-tuple-element.22.inv_ref, f32[8,128,128]{2,1,0:T(8,128)} %get-tuple-element.23.cross_ref, ...), custom_call_target="tpu_custom_call" | custom-call | tf_op jit(solution)/shard_map/block_tokens/pallas_call | solution.py:268
  182.9 7.8 %block_tokens.2 = (f32[8,128,128]{2,1,0:T(8,128)}, f32[8,128,128]{2,1,0:T(8,128)}) custom-call(bf16[128,2048]{1,0:T(8,128)(2,1)} %q_ref.3, bf16[128,2,2048]{2,1,0:T(2,128)(2,1)} %k_ref.7, bf16[128,2,2048]{2,1,0:T(2,128)(2,1)} %v_ref.7, f32[8,256,128]{2,1,0:T(8,128)} %get-tuple-element.17.inv_ref, f32[8,128,128]{2,1,0:T(8,128)} %get-tuple-element.18.cross_ref, ...), custom_call_target="tpu_custom_call" | custom-call | tf_op jit(solution)/shard_map/block_tokens/pallas_call | solution.py:268
  190.6 8.6 %all-to-all-done.5.state_ref = f32[16,128,128]{2,1,0:T(8,128)S(1)} async-done(((f32[16,128,128]{2,1,0:T(8,128)}), f32[16,128,128]{2,1,0:T(8,128)S(1)}, u32[]{:S(2)}, u32[]{:S(2)}) %all-to-all-start.5) | async-done | bytes 1048608 | tf_op jit(solution)/shard_map/all_to_all | solution.py:482
  199.3 4.3 %finish.1 = bf16[128,2048]{1,0:T(8,128)(2,1)} custom-call(f32[8,128,128]{2,1,0:T(8,128)} %get-tuple-element.20.l0, f32[8,128,128]{2,1,0:T(8,128)} %get-tuple-element.21.c0, f32[8,128,128]{2,1,0:T(8,128)} %get-tuple-element.25.l1, f32[8,128,128]{2,1,0:T(8,128)} %get-tuple-element.26.c1, f32[16,128,128]{2,1,0:T(8,128)S(1)} %all-to-all-done.5.state_ref, ...), custom_call_target="tpu_custom_call" | custom-call | tf_op jit(solution)/shard_map/finish/pallas_call | solution.py:441
Async XLA Ops:
  9.5 31.6 %all-to-all-start.1 = ((f32[8,128,256]{2,1,0:T(8,128)}), f32[8,128,256]{2,1,0:T(8,128)S(1)}, u32[]{:S(2)}, u32[]{:S(2)}) async-start(f32[8,128,256]{2,1,0:T(8,128)} %get-tuple-element.28), calls=%async_computation.1 | async-start | bytes 2097152 | tf_op jit(solution)/shard_map/all_to_all | solution.py:466
  41.1 28.7 %all-to-all-start = ((f32[8,128,256]{2,1,0:T(8,128)}), f32[8,128,256]{2,1,0:T(8,128)S(1)}, u32[]{:S(2)}, u32[]{:S(2)}) async-start(f32[8,128,256]{2,1,0:T(8,128)} %get-tuple-element.27), calls=%async_computation | async-start | bytes 2097152 | tf_op jit(solution)/shard_map/all_to_all | solution.py:466
  71.3 42.2 %all-to-all-start.2 = ((f32[4,128,256]{2,1,0:T(8,128)}), f32[4,128,256]{2,1,0:T(8,128)S(1)}, u32[]{:S(2)}, u32[]{:S(2)}) async-start(f32[4,128,256]{2,1,0:T(8,128)} %quad_total.3), calls=%async_computation.2 | async-start | bytes 1048576 | tf_op jit(solution)/shard_map/all_to_all | solution.py:470
  139.0 4.9 %collective-permute-start = (f32[16,128,128]{2,1,0:T(8,128)}, f32[16,128,128]{2,1,0:T(8,128)}, u32[]{:S(2)}, u32[]{:S(2)}) collective-permute-start(f32[16,128,128]{2,1,0:T(8,128)} %all_to_all.30.mine_ref), channel_id=1, source_target_pairs={{0,16},{16,0},{1,17},{17,1},{2,18},{18,2},{3,19},{19,3},{4,20},{20... | collective-permute-start | bytes 3145736 | tf_op jit(solution)/shard_map/ppermute | solution.py:477
  170.3 29.0 %all-to-all-start.5 = ((f32[16,128,128]{2,1,0:T(8,128)}), f32[16,128,128]{2,1,0:T(8,128)S(1)}, u32[]{:S(2)}, u32[]{:S(2)}) async-start(f32[16,128,128]{2,1,0:T(8,128)} %spread.1), calls=%async_computation.5 | async-start | bytes 2097152 | tf_op jit(solution)/shard_map/all_to_all | solution.py:482
